TPU v7x, 256 devices: a whole 4x4x8 slice. The times are simulated.
256 devices in a mesh: outer: 32 (over y_lo, z, core), inner: 8 (over y_hi, x).
Axes of the slice: x: 4, y: 4 (y_hi: 2, y_lo: 2; y = y_hi * 2 + y_lo), z: 8, core: 2. Of those that a mesh axis runs over, the one named last changes fastest.
Arguments:
- tokens: bfloat16 [180224, 4096], P(('outer', 'inner')), may hold values from -24 to 24
- weight: bfloat16 [4096, 512], P(('outer', 'inner')), may hold values from -0.09375 to 0.09375
- bias: float32 [512], replicated, may hold values from -5 to 5
- grad_values: bfloat16 [180224, 512], P(('outer', 'inner')), may hold values from -6 to 6
Outputs:
- values: bfloat16 [180224, 512], P(('outer', 'inner'))
- grad_tokens: bfloat16 [180224, 4096], P(('outer', 'inner'))
- grad_weight: float32 [4096, 512], P(('outer', 'inner'))
- grad_bias: float32 [512], replicated
All inputs are finite; a program needn't handle non-finite values.
Results may differ from a plain program's by a relative error of at most 0.0005.
Values may be sent and summed in bfloat16 or wider, within the bound.
A program may use at most 128 MiB of HBM per device.

v0:
```python
import jax
import jax.numpy as jnp
from jax import lax
from jax.sharding import PartitionSpec as P


def forward_add(tokens_three, piece):
    return jnp.einsum("tok,okh->th", tokens_three, piece, preferred_element_type=jnp.float32)


def backward_put(grad_values, piece):
    part = jnp.einsum("th,okh->tok", grad_values, piece, preferred_element_type=jnp.float32)
    return part


def shards(tokens, weight, bias, grad_values):
    n_outer = lax.axis_size("outer")
    n_inner = lax.axis_size("inner")
    tok_rows = tokens.shape[0]
    width = tokens.shape[1]
    feats = weight.shape[1]
    shard_rows = weight.shape[0]
    scale = 1.0 / jnp.sqrt(jnp.float32(tok_rows * n_outer * n_inner))
    tokens_three = tokens.reshape(tok_rows, n_outer, n_inner * shard_rows)
    secondary = lax.all_gather(weight, "outer", axis=0, tiled=True).reshape(
        n_outer, shard_rows, feats
    )
    projected = forward_add(tokens_three, lax.all_gather(secondary, "inner", axis=1, tiled=True))
    grad_three = backward_put(grad_values, lax.all_gather(secondary, "inner", axis=1, tiled=True))
    grad_full = grad_three.reshape(tok_rows, width)
    values = (projected + bias).astype(jnp.bfloat16)
    grad_tokens = grad_full.astype(jnp.bfloat16)
    tokens_four = tokens.reshape(tok_rows, n_outer, n_inner, shard_rows)
    partial_sum = lax.psum_scatter(
        jnp.einsum("toir,th->iorh", tokens_four, grad_values, preferred_element_type=jnp.float32)
        * scale,
        "inner",
        scatter_dimension=0,
        tiled=True,
    )
    grad_weight = lax.psum_scatter(partial_sum, "outer", scatter_dimension=1, tiled=True).reshape(
        shard_rows, feats
    )
    grad_bias = lax.psum(
        jnp.sum(grad_values.astype(jnp.float32), axis=0) * scale, ("outer", "inner")
    )
    return (values, grad_tokens, grad_weight, grad_bias)


def solution(mesh):
    in_specs = (
        P(("outer", "inner"), None),
        P(("outer", "inner"), None),
        P(),
        P(("outer", "inner"), None),
    )
    out_specs = (
        P(("outer", "inner"), None),
        P(("outer", "inner"), None),
        P(("outer", "inner"), None),
        P(),
    )
    return jax.shard_map(shards, mesh=mesh, in_specs=in_specs, out_specs=out_specs, check_vma=False)
```

profile of v0, /device:TPU:8, one launch (start us, length us, event | category | flops | bytes accessed | tf_op | source)
XLA Modules:
  0.0 353.1 jit_solution(10234715800456797534)
XLA Ops:
  7.2 0.0 copy-start
  7.2 0.0 reduce-scatter.3.cloned.1.call-start
  7.2 8.4 %copy.16 = bf16[704,4096]{0,1:T(8,128)(2,1)} copy(bf16[704,4096]{1,0:T(8,128)(2,1)} %param.4) | data formatting | bytes 11534336 | tf_op args[0]
  15.6 0.0 copy-done
  15.6 13.5 %multiply_bitcast_fusion = f32[8,32,16,512]{3,1,2,0:T(8,128)} fusion(bf16[704,32,8,16]{0,3,2,1:T(8,128)(2,1)} %bitcast.35, bf16[704,512]{1,0:T(8,128)(2,1)S(1)} %copy-done), kind=kOutput, calls=%fused_computation | convolution fusion | flops 2954887168 | bytes 14876672 | tf_op jit(solution)/shard_map/toir,th->iorh/dot_general | solution.py:35
  29.1 0.0 copy-start.1
  29.1 0.0 reduce-scatter.3.cloned.1.call-update
  29.2 0.0 all-gather.2.cloned.1.call-start
  29.2 0.6 copy-done.1
  29.9 40.5 %all_gather.7 = bf16[512,512]{1,0:T(8,128)(2,1)} all-gather(bf16[16,512]{1,0:T(8,128)(2,1)S(1)} %copy-done.1), channel_id=1, replica_groups=mesh['outer'=32,'inner'=8] {'outer'}, dimensions={0}, use_global_device_ids=true | all-gather | bytes 540672 | tf_op jit(solution)/shard_map/all_gather | solution.py:25
  70.4 0.0 all-gather.2.cloned.1.call-update
  70.4 0.0 reduce-scatter.5.cloned.1.call-start
  70.5 80.5 %reduce-scatter.3.cloned.1.call-done = f32[1,32,16,512]{3,1,2,0:T(8,128)} async-done(((f32[8,32,16,512]{3,1,2,0:T(8,128)}), f32[1,32,16,512]{3,1,2,0:T(8,128)}) %reduce-scatter.3.cloned.1.call-update) | async-done | bytes 1048592 | tf_op jit(solution)/shard_map/reduce_scatter | solution.py:34
  151.0 2.8 copy.18
  153.8 0.0 reduce-scatter.5.cloned.1.call-update
  153.8 0.2 convert_reduce_fusion
  153.9 79.0 %psum.7 = f32[512]{0:T(512)} all-reduce(f32[512]{0:T(512)S(1)} %broadcast_multiply_fusion), channel_id=1, replica_groups=mesh['outer'=32,'inner'=8] {'outer','inner'}, use_global_device_ids=true, to_apply=%region_3.0 | all-reduce | flops 512 | bytes 4096 | tf_op jit(solution)/shard_map/psum | solution.py:44
  232.9 0.0 all-gather.2.cloned.1.call-done
  232.9 5.6 %convert_bitcast_fusion = bf16[32,88,8,128]{3,2,1,0:T(8,128)(2,1)S(1)} fusion(bf16[32,128,512]{2,1,0:T(8,128)(2,1)} %all-gather.2.cloned.1.call-done, bf16[704,512]{1,0:T(8,128)(2,1)S(1)} %copy-done), kind=kOutput, calls=%fused_computation.7 | convolution fusion | flops 2955673600 | bytes 10682368 | tf_op jit(solution)/shard_map/th,okh->tok/dot_general | solution.py:12
  238.5 0.0 copy-start.2
  238.5 0.0 copy-start.3
  238.5 4.2 %copy.35 = bf16[32,88,8,128]{3,2,0,1:T(8,128)(2,1)} copy(bf16[32,88,8,128]{3,2,1,0:T(8,128)(2,1)S(1)} %convert_bitcast_fusion) | data formatting | bytes 11534336 | tf_op jit(solution)/shard_map/convert_element_type | solution.py:32
  242.7 0.0 copy-done.2
  242.7 0.0 copy-done.3
  242.7 6.0 %add_convert_fusion = bf16[704,512]{1,0:T(8,128)(2,1)} fusion(bf16[32,128,512]{2,1,0:T(8,128)(2,1)S(1)} %copy-done.2, f32[512]{0:T(512)S(1)} %copy-done.3, bf16[704,4096]{1,0:T(8,128)(2,1)} %param.4), kind=kOutput, calls=%fused_computation.10 | convolution fusion | flops 2953510912 | bytes 10684416 | tf_op jit(solution)/shard_map/tok,okh->th/dot_general | solution.py:8
  248.7 97.8 %reduce-scatter.5.cloned.1.call-done = f32[1,1,16,512]{3,2,0,1:T(8,128)} async-done(((f32[1,32,16,512]{3,2,0,1:T(8,128)}), f32[1,1,16,512]{3,2,0,1:T(8,128)}) %reduce-scatter.5.cloned.1.call-update) | async-done | bytes 32784 | tf_op jit(solution)/shard_map/reduce_scatter | solution.py:41
  (1 shorter events, 0.0 us)
Async XLA Ops:
  7.2 8.4 %copy-start = (bf16[704,512]{1,0:T(8,128)(2,1)S(1)}, bf16[704,512]{1,0:T(8,128)(2,1)}, u32[]{:S(2)}) copy-start(bf16[704,512]{1,0:T(8,128)(2,1)} %param.7) | copy-start | bytes 2162692
  7.2 143.8 %reduce-scatter.3.cloned.1.call-start = ((), (), s32[]{:S(2)}) async-start(), calls=%async_computation.3 | async-start | bytes 9437184 | tf_op jit(solution)/shard_map/reduce_scatter | solution.py:34
  29.1 0.7 copy-start.1
  29.2 203.7 %all-gather.2.cloned.1.call-start = ((), (), s32[]{:S(2)}) async-start(), calls=%async_computation.2 | async-start | bytes 4718592 | tf_op jit(solution)/shard_map/all_gather | solution.py:28
  70.4 276.1 %reduce-scatter.5.cloned.1.call-start = ((), (), s32[]{:S(2)}) async-start(), calls=%async_computation.4 | async-start | bytes 1081344 | tf_op jit(solution)/shard_map/reduce_scatter | solution.py:41
  238.5 4.2 %copy-start.2 = (bf16[32,128,512]{2,1,0:T(8,128)(2,1)S(1)}, bf16[32,128,512]{2,1,0:T(8,128)(2,1)}, u32[]{:S(2)}) copy-start(bf16[32,128,512]{2,1,0:T(8,128)(2,1)} %all-gather.2.cloned.1.call-done) | copy-start | bytes 12582916
  238.5 4.2 %copy-start.3 = (f32[512]{0:T(512)S(1)}, f32[512]{0:T(512)}, u32[]{:S(2)}) copy-start(f32[512]{0:T(512)} %param.6) | copy-start | bytes 6148
Sparse Core Ops, SparseCore 0:
  29.3 121.6 reduce-scatter.2
  153.6 75.0 all-gather.1
  231.8 114.7 reduce-scatter.4
where the time goes:
time: 355 us; the launch traced here: 353 us
  waiting for transfers between devices  178 us (50%)
  blocking collectives  120 us (34%)
  matrix products  25.1 us (7%)
  local copies, waits for them, and re-layouts  16 us (5%)
  between operations  13.8 us (4%)
    reduce_scatter x1, waiting for transfers between devices, shards(): lax.psum_scatter(partial_sum, 'outer', scatter_dimension=1, tiled=True)  97.8 us
    reduce_scatter x1, waiting for transfers between devices, shards(): lax.psum_scatter(jnp.einsum('toir,th->iorh', tokens_four, grad_values, pr...  80.5 us
    psum x1, blocking collectives, shards(): lax.psum(jnp.sum(grad_values.astype(jnp.float32), axis=0) * scale, ('oute...  79 us
    all_gather x1, blocking collectives, shards(): lax.all_gather(weight, 'outer', axis=0, tiled=True)  40.5 us
    dot_general x1, matrix products, shards(): jnp.einsum('toir,th->iorh', tokens_four, grad_values, preferred_element_t...  13.5 us
    unnamed x9, local copies, waits for them, and re-layouts  9.04 us
  transfers between devices with their start and end apart: 3, of which 2 were waited for; matrix products, arithmetic and copies ran while one was open for 5% of the time, Pallas kernels for 0%

commit v1 on v0

v1 whole, which is shorter than its diff:
```python
import functools

import jax
import jax.numpy as jnp
from jax import lax
from jax.experimental import pallas as pl
from jax.experimental.pallas import tpu as pltpu
from jax.sharding import PartitionSpec as P

X, Y, Z = 4, 4, 8
MESH = pl.DeviceIdType.MESH
F32, BF16 = jnp.float32, jnp.bfloat16
N_SEM = 170
LOW = (pl.ds(0, 4), pl.ds(0, 2), pl.ds(2, 1))
HIGH = (pl.ds(4, 4), pl.ds(0, 1), pl.ds(1, 2))
A_PARTS = ((pl.ds(0, 4), pl.ds(0, 2), pl.ds(0, 2)), (pl.ds(4, 4), pl.ds(0, 1), pl.ds(0, 1)))
B_PARTS = ((pl.ds(0, 4), pl.ds(2, 1), pl.ds(1, 1)), (pl.ds(4, 4), pl.ds(1, 2), pl.ds(0, 2)))
C_GROUP = pl.ds(3, 1)


def kernel(
    scale,
    tok_hbm, w_hbm, bias_ref, gv_hbm,
    val_hbm, gt_hbm, gw_ref, gb_ref,
    tok, gv, wb, gall, gr, acc, gto, valo,
    rx1, ry1, sa, sb, ry2, rx2, s2, rz3, cp, cm, sc, rc2, sc2, rc3,
    bb, bx, by, bz,
    ssem, rsem, dsem, drsem, lsem, osem,
):
    outer = lax.axis_index("outer")
    inner = lax.axis_index("inner")
    c = lax.rem(outer, 2)
    z = lax.rem(outer // 2, Z)
    yl = outer // (2 * Z)
    x = lax.rem(inner, X)
    yh = inner // X
    y = yh * 2 + yl

    def dev(px, py, pz, pc):
        return {
            "outer": (lax.rem(py, 2) * Z + pz) * 2 + pc,
            "inner": (py // 2) * X + px,
        }

    def at_x(k):
        p = lax.rem(x + k + X, X)
        return p, dev(p, y, z, c)

    def at_y(k):
        p = lax.rem(y + k + Y, Y)
        return p, dev(x, p, z, c)

    def at_z(k):
        p = lax.rem(z + k + Z, Z)
        return p, dev(x, y, p, c)

    sibling = dev(x, y, z, 1 - c)
    yhl = lambda p: (p // 2, lax.rem(p, 2))
    count = [0]
    sends = []

    def send(src, dst, to):
        i = count[0]
        count[0] += 1
        cp_ = pltpu.make_async_remote_copy(
            src_ref=src, dst_ref=dst, send_sem=ssem.at[i], recv_sem=rsem.at[i],
            device_id=to, device_id_type=MESH,
        )
        cp_.start()
        sends.append(cp_)
        return i

    def got(i, dst):
        pltpu.make_async_remote_copy(
            src_ref=dst, dst_ref=dst, send_sem=ssem.at[i], recv_sem=rsem.at[i],
            device_id=sibling, device_id_type=MESH,
        ).wait_recv()

    half = (1 - yl, yl)
    tok_in = []
    for h in range(2):
        cols = pl.ds(pl.multiple_of(half[h] * 2048, 2048), 2048)
        tok_in.append(pltpu.make_async_copy(tok_hbm.at[:, cols], tok.at[:, cols], lsem.at[h]))
    gv_in = pltpu.make_async_copy(gv_hbm, gv, lsem.at[2])
    w_in = [
        pltpu.make_async_copy(
            w_hbm.at[:, pl.ds(g * 128, 128)], wb.at[yl, z, c, yh, x, g], lsem.at[3 + g]
        )
        for g in range(4)
    ]
    for cp_ in w_in:
        cp_.start()
    gv_in.start()
    for cp_ in tok_in:
        cp_.start()

    barrier = pltpu.get_barrier_semaphore()
    peers = [at_x(k)[1] for k in range(1, X)] + [at_y(k)[1] for k in range(1, Y)]
    peers += [at_z(k)[1] for k in range(1, Z)] + [sibling]
    for p in peers:
        pl.semaphore_signal(barrier, inc=1, device_id=p, device_id_type=MESH)
    for cp_ in w_in:
        cp_.wait()
    pl.semaphore_wait(barrier, len(peers))

    ag1 = []
    for k in range(1, Z):
        ref = wb.at[yl, z, c, yh, x, pl.ds(0, 3)]
        ag1.append(send(ref, ref, at_z(k)[1]))
    agc1 = []
    for k in range(1, Y):
        ref = wb.at[yl, z, c, yh, x, C_GROUP]
        agc1.append(send(ref, ref, at_y(k)[1]))

    gv_in.wait()
    gvf = gv[...].astype(F32)
    bb[c] = jnp.sum(gvf.reshape(-1, 8, 512), axis=0)
    bias_core = send(bb.at[c], bb.at[c], sibling)

    def d2d(h, i):
        return pltpu.make_async_remote_copy(
            src_ref=gall.at[1 - c, half[h], i], dst_ref=gr.at[half[h], i],
            send_sem=dsem.at[h * Z + i], recv_sem=drsem.at[h * Z + i],
            device_id=sibling, device_id_type=MESH,
        )

    def grads(h, lo, hi):
        @pl.loop(lo, hi)
        def _(i):
            col = pl.multiple_of((half[h] * Z + i) * 256, 256)
            part = lax.dot_general(
                tok[:, pl.ds(col, 256)], gv[...], (((0,), (0,)), ((), ())),
                preferred_element_type=F32,
            ) * scale
            for g in range(4):
                gall[:, half[h], i, :, :, g] = part[:, g * 128:(g + 1) * 128].reshape(
                    2, 2, X, 16, 128
                )
            d2d(h, i).start()

    tok_in[0].wait()
    grads(0, 0, Z)

    for k in range(1, Z):
        got(ag1[k - 1], wb.at[yl, at_z(-k)[0], c, yh, x, pl.ds(0, 3)])
    ag2a, ag2b, agc2 = {}, {}, {}
    for k in range(1, Y):
        for q, (zs, gs, _) in enumerate(A_PARTS):
            ref = wb.at[yl, zs, c, yh, x, gs]
            ag2a[k, q] = send(ref, ref, at_y(k)[1])
    for k in range(1, X):
        for q, (zs, gs, _) in enumerate(B_PARTS):
            ref = wb.at[yl, zs, c, yh, x, gs]
            ag2b[k, q] = send(ref, ref, at_x(k)[1])
    for k in range(1, Y):
        ph, pw = yhl(at_y(-k)[0])
        got(agc1[k - 1], wb.at[pw, z, c, ph, x, C_GROUP])
    for k in range(1, X):
        ref = wb.at[:, z, c, :, x, C_GROUP]
        agc2[k] = send(ref, ref, at_x(k)[1])

    tok_in[1].wait()
    grads(1, 0, Z)

    fwd = []

    def relay(ref):
        fwd.append((send(ref, ref, sibling), ref))

    for k in range(1, Y):
        ph, pw = yhl(at_y(-k)[0])
        for q, (zs, gs, _) in enumerate(A_PARTS):
            got(ag2a[k, q], wb.at[pw, zs, c, ph, x, gs])
    a_slab = lambda p, q, cc: wb.at[:, A_PARTS[q][0], cc, :, p, A_PARTS[q][1]]
    b_slab = lambda p, q, cc: wb.at[yhl(p)[1], B_PARTS[q][0], cc, yhl(p)[0], :, B_PARTS[q][1]]
    c_slab = lambda p, cc: wb.at[:, p, cc, :, :, C_GROUP]
    ag3a, ag3b, agp, agm = {}, {}, {}, {}
    for k in range(1, X):
        for q in range(2):
            ref = a_slab(x, q, c)
            ag3a[k, q] = send(ref, ref, at_x(k)[1])
    for k in range(1, X):
        for q, (zs, gs, _) in enumerate(B_PARTS):
            got(ag2b[k, q], wb.at[yl, zs, c, yh, at_x(-k)[0], gs])
    for k in range(1, Y):
        for q in range(2):
            ref = b_slab(y, q, c)
            ag3b[k, q] = send(ref, ref, at_y(k)[1])
    for k in range(1, X):
        got(agc2[k], wb.at[:, z, c, :, at_x(-k)[0], C_GROUP])

    def gather_ring(s):
        ref = c_slab(at_z(1 - s)[0], c)
        agp[s] = send(ref, ref, at_z(1)[1])
        if s < 4:
            ref = c_slab(at_z(s - 1)[0], c)
            agm[s] = send(ref, ref, at_z(-1)[1])

    def gather_ring_got(s):
        got(agp[s], c_slab(at_z(-s)[0], c))
        if s < 4:
            got(agm[s], c_slab(at_z(s)[0], c))

    gather_ring(1)
    d2d_c = {}

    def relay_all(table, key, mk):
        table[key] = send(mk(c), mk(c), sibling)

    for q in range(2):
        relay_all(d2d_c, ("a", 0, q), lambda cc: a_slab(x, q, cc))
        relay_all(d2d_c, ("b", 0, q), lambda cc: b_slab(y, q, cc))
    relay_all(d2d_c, ("c", 0, 0), lambda cc: c_slab(z, cc))

    rsa, rsb, rsp, rsm = {}, {}, {}, {}

    def combine(h):
        @pl.loop(0, Z)
        def _(i):
            pltpu.make_async_remote_copy(
                src_ref=gr.at[half[h], i], dst_ref=gr.at[half[h], i],
                send_sem=dsem.at[h * Z + i], recv_sem=drsem.at[h * Z + i],
                device_id=sibling, device_id_type=MESH,
            ).wait_recv()
            gall[c, half[h], i] = gall[c, half[h], i] + gr[half[h], i]

    def ring_first(h):
        rsp[1, h] = send(gall.at[c, half[h], at_z(4)[0], :, :, C_GROUP], cp.at[0, h], at_z(1)[1])
        rsm[1, h] = send(gall.at[c, half[h], at_z(-3)[0], :, :, C_GROUP], cm.at[0, h], at_z(-1)[1])

    def ring_next(s, h):
        got(rsp[s - 1, h], cp.at[s - 2, h])
        cp[s - 2, h] = cp[s - 2, h] + gall[c, half[h], at_z(5 - s)[0], :, :, C_GROUP]
        rsp[s, h] = send(cp.at[s - 2, h], cp.at[s - 1, h], at_z(1)[1])
        if s < 4:
            got(rsm[s - 1, h], cm.at[s - 2, h])
            cm[s - 2, h] = cm[s - 2, h] + gall[c, half[h], at_z(s - 4)[0], :, :, C_GROUP]
            rsm[s, h] = send(cm.at[s - 2, h], cm.at[s - 1, h], at_z(-1)[1])

    def scatter_first(h):
        ring_first(h)
        for k in range(1, X):
            p, to = at_x(k)
            for q, (zs, gs, ls) in enumerate(A_PARTS):
                rsa[k, q, h] = send(
                    gall.at[c, half[h], zs, :, p, gs], rx1.at[x, half[h], zs, :, ls], to
                )
        for k in ((1, 3), (2,))[h]:
            p, to = at_y(k)
            ph, _ = yhl(p)
            for q, (zs, gs, ls) in enumerate(B_PARTS):
                rsb[k, q] = send(
                    gall.at[c, half[h], zs, ph, :, gs], ry1.at[y, zs, :, ls], to
                )

    combine(0)
    scatter_first(0)
    combine(1)
    scatter_first(1)

    got(bias_core, bb.at[1 - c])
    bx[x] = bb[0] + bb[1]
    bias_x = [send(bx.at[x], bx.at[x], at_x(k)[1]) for k in range(1, X)]

    for s in range(1, 5):
        gather_ring_got(s)
        if s < 4:
            gather_ring(s + 1)
        relay_all(d2d_c, ("c", -s, 0), lambda cc: c_slab(at_z(-s)[0], cc))
        if s < 4:
            relay_all(d2d_c, ("c", s, 0), lambda cc: c_slab(at_z(s)[0], cc))
        if s < 4:
            for q in range(2):
                got(ag3a[s, q], a_slab(at_x(-s)[0], q, c))
                relay_all(d2d_c, ("a", s, q), lambda cc: a_slab(at_x(-s)[0], q, cc))
                got(ag3b[s, q], b_slab(at_y(-s)[0], q, c))
                relay_all(d2d_c, ("b", s, q), lambda cc: b_slab(at_y(-s)[0], q, cc))
    for h in range(2):
        ring_next(2, h)
    for (kind, k, q), i in d2d_c.items():
        if kind == "a":
            got(i, a_slab(at_x(-k)[0], q, 1 - c))
        elif kind == "b":
            got(i, b_slab(at_y(-k)[0], q, 1 - c))
        else:
            got(i, c_slab(at_z(k)[0], 1 - c))

    acc[...] = jnp.broadcast_to(bias_ref[...], acc.shape)

    def product_out(j):
        cols = pl.ds(pl.multiple_of(j * 512, 512), 512)
        return pltpu.make_async_copy(gto.at[:, cols], gt_hbm.at[:, cols], osem.at[j])

    def products(lo, hi):
        @pl.loop(lo, hi)
        def _(j):
            zz = pl.multiple_of(lax.rem(j, 4) * 2, 2)
            w = jnp.concatenate(
                [wb[j // 4, pl.ds(zz, 2), :, :, :, g].reshape(512, 128) for g in range(4)], axis=1
            )
            cols = pl.ds(pl.multiple_of(j * 512, 512), 512)
            gto[:, cols] = lax.dot_general(
                gv[...], w, (((1,), (1,)), ((), ())), preferred_element_type=F32
            ).astype(BF16)
            product_out(j).start()
            acc[...] += jnp.dot(tok[:, cols], w, preferred_element_type=F32)

    products(0, 3)
    for h in range(2):
        ring_next(3, h)
    for k in range(1, X):
        got(bias_x[k - 1], bx.at[at_x(-k)[0]])
    by[y] = (bx[0] + bx[1]) + (bx[2] + bx[3])
    bias_y = [send(by.at[y], by.at[y], at_y(k)[1]) for k in range(1, Y)]
    products(3, 6)
    for h in range(2):
        ring_next(4, h)
    for k in range(1, Y):
        got(bias_y[k - 1], by.at[at_y(-k)[0]])
    bz[z] = (by[0] + by[1]) + (by[2] + by[3])
    bias_z = [send(bz.at[z], bz.at[z], at_z(k)[1]) for k in range(1, Z)]
    products(6, 8)
    valo[...] = acc[...].astype(BF16)
    val_out = pltpu.make_async_copy(valo, val_hbm, osem.at[8])
    val_out.start()

    rs2a, rs2b, rsc2 = {}, {}, {}
    for h in range(2):
        for k in range(1, X):
            for q, (zs, gs, ls) in enumerate(A_PARTS):
                got(rsa[k, q, h], rx1.at[at_x(-k)[0], half[h], zs, :, ls])
        for q, (zs, gs, ls) in enumerate(A_PARTS):
            total = gall[c, half[h], zs, :, x, gs]
            for k in range(1, X):
                total = total + rx1[at_x(-k)[0], half[h], zs, :, ls]
            sa[half[h], zs, :, ls] = total
        for k in ((1, 3), (2,))[h]:
            p, to = at_y(k)
            ph, _ = yhl(p)
            for q, (zs, gs, ls) in enumerate(A_PARTS):
                rs2a[k, q] = send(sa.at[half[h], zs, ph, ls], ry2.at[y, zs, ls], to)
    for k in range(1, Y):
        for q, (zs, gs, ls) in enumerate(B_PARTS):
            got(rsb[k, q], ry1.at[at_y(-k)[0], zs, :, ls])
    for q, (zs, gs, ls) in enumerate(B_PARTS):
        total = gall[c, yl, zs, yh, :, gs]
        for k in range(1, Y):
            total = total + ry1[at_y(-k)[0], zs, :, ls]
        sb[zs, :, ls] = total
    for k in range(1, X):
        p, to = at_x(k)
        for q, (zs, gs, ls) in enumerate(B_PARTS):
            rs2b[k, q] = send(sb.at[zs, p, ls], rx2.at[x, zs, ls], to)
    for h in range(2):
        got(rsp[4, h], cp.at[3, h])
        got(rsm[3, h], cm.at[2, h])
        sc[half[h]] = gall[c, half[h], z, :, :, 3] + cp[3, h, :, :, 0] + cm[2, h, :, :, 0]
    for k in range(1, X):
        p, to = at_x(k)
        rsc2[k] = send(sc.at[:, :, p], rc2.at[x], to)

    for k in range(1, Y):
        for q, (zs, gs, ls) in enumerate(A_PARTS):
            got(rs2a[k, q], ry2.at[at_y(-k)[0], zs, ls])
    for q, (zs, gs, ls) in enumerate(A_PARTS):
        total = sa[yl, zs, yh, ls]
        for k in range(1, Y):
            total = total + ry2[at_y(-k)[0], zs, ls]
        s2[zs, gs] = total
    for k in range(1, X):
        for q, (zs, gs, ls) in enumerate(B_PARTS):
            got(rs2b[k, q], rx2.at[at_x(-k)[0], zs, ls])
    for q, (zs, gs, ls) in enumerate(B_PARTS):
        total = sb[zs, x, ls]
        for k in range(1, X):
            total = total + rx2[at_x(-k)[0], zs, ls]
        s2[zs, gs] = total
    rs3 = {}
    for k in range(1, Z):
        p, to = at_z(k)
        rs3[k] = send(s2.at[p], rz3.at[z], to)
    for k in range(1, X):
        got(rsc2[k], rc2.at[at_x(-k)[0]])
    total = sc[:, :, x]
    for k in range(1, X):
        total = total + rc2[at_x(-k)[0]]
    sc2[...] = total
    rsc3 = {}
    for k in range(1, Y):
        p, to = at_y(k)
        ph, pw = yhl(p)
        rsc3[k] = send(sc2.at[pw, ph], rc3.at[y], to)

    for k in range(1, Z):
        got(bias_z[k - 1], bz.at[at_z(-k)[0]])
    total = bz[0]
    for k in range(1, Z):
        total = total + bz[k]
    gb_ref[...] = jnp.sum(total, axis=0, keepdims=True) * scale
    for k in range(1, Y):
        got(rsc3[k], rc3.at[at_y(-k)[0]])
    total = sc2[yl, yh]
    for k in range(1, Y):
        total = total + rc3[at_y(-k)[0]]
    gw_ref[:, pl.ds(384, 128)] = total
    for k in range(1, Z):
        got(rs3[k], rz3.at[at_z(-k)[0]])
    total = s2[z]
    for k in range(1, Z):
        total = total + rz3[at_z(-k)[0]]
    for g in range(3):
        gw_ref[:, pl.ds(g * 128, 128)] = total[g]

    val_out.wait()
    for j in range(8):
        product_out(j).wait()
    for cp_ in sends:
        cp_.wait_send()

    @pl.loop(0, 2 * Z)
    def _(i):
        pltpu.make_async_remote_copy(
            src_ref=gr.at[0, 0], dst_ref=gr.at[0, 0], send_sem=dsem.at[i], recv_sem=drsem.at[i],
            device_id=sibling, device_id_type=MESH,
        ).wait_send()
    assert count[0] <= N_SEM, count[0]


def shards(tokens, weight, bias, grad_values):
    rows, width = tokens.shape
    feats = weight.shape[1]
    n = lax.axis_size("outer") * lax.axis_size("inner")
    scale = float(1.0 / (rows * n) ** 0.5)
    anyspace = pl.BlockSpec(memory_space=pl.ANY)
    vmem = pl.BlockSpec(memory_space=pltpu.VMEM)
    tile = (16, 128)
    scratch = [
        ((rows, width), BF16),
        ((rows, feats), BF16),
        ((2, Z, 2, 2, X, 4) + tile, BF16),
        ((2, 2, Z, 2, X, 4) + tile, F32),
        ((2, Z, 2, X, 4) + tile, F32),
        ((rows, feats), F32),
        ((rows, width), BF16),
        ((rows, feats), BF16),
        ((X, 2, Z, 2, 2) + tile, F32),
        ((Y, Z, X, 2) + tile, F32),
        ((2, Z, 2, 2) + tile, F32),
        ((Z, X, 2) + tile, F32),
        ((Y, Z, 2) + tile, F32),
        ((X, Z, 2) + tile, F32),
        ((Z, 3) + tile, F32),
        ((Z, 3) + tile, F32),
        ((4, 2, 2, X, 1) + tile, F32),
        ((3, 2, 2, X, 1) + tile, F32),
        ((2, 2, X) + tile, F32),
        ((X, 2, 2) + tile, F32),
        ((2, 2) + tile, F32),
        ((Y,) + tile, F32),
        ((2, 8, feats), F32),
        ((X, 8, feats), F32),
        ((Y, 8, feats), F32),
        ((Z, 8, feats), F32),
    ]
    dma = pltpu.SemaphoreType.DMA
    values, grad_tokens, grad_weight, grad_bias = pl.pallas_call(
        functools.partial(kernel, scale),
        out_shape=(
            jax.ShapeDtypeStruct((rows, feats), BF16),
            jax.ShapeDtypeStruct((rows, width), BF16),
            jax.ShapeDtypeStruct(weight.shape, F32),
            jax.ShapeDtypeStruct((1, feats), F32),
        ),
        in_specs=[anyspace, anyspace, vmem, anyspace],
        out_specs=(anyspace, anyspace, vmem, vmem),
        scratch_shapes=[pltpu.VMEM(s, d) for s, d in scratch]
        + [dma((N_SEM,)), dma((N_SEM,)), dma((2 * Z,)), dma((2 * Z,)), dma((8,)), dma((16,))],
        compiler_params=pltpu.CompilerParams(
            collective_id=0, has_side_effects=True, vmem_limit_bytes=60 * 1024 * 1024
        ),
        cost_estimate=pl.CostEstimate(
            flops=6 * rows * width * feats, bytes_accessed=4 * rows * width, transcendentals=0
        ),
    )(tokens, weight, bias.reshape(1, feats), grad_values)
    return values, grad_tokens, grad_weight, grad_bias.reshape(feats)


def solution(mesh):
    in_specs = (
        P(("outer", "inner"), None),
        P(("outer", "inner"), None),
        P(),
        P(("outer", "inner"), None),
    )
    out_specs = (
        P(("outer", "inner"), None),
        P(("outer", "inner"), None),
        P(("outer", "inner"), None),
        P(),
    )
    return jax.shard_map(shards, mesh=mesh, in_specs=in_specs, out_specs=out_specs, check_vma=False)
```

time: 355 us -> 78.6 us (0.22)
  waiting for transfers between devices: 178 us -> 0 us
  blocking collectives: 120 us -> 0 us
  Pallas kernels: 0 us -> 67.8 us
  matrix products: 25.1 us -> 0 us
  between operations: 13.8 us -> 0.64 us
  local copies, waits for them, and re-layouts: 16 us -> 9.11 us
    reduce_scatter x2 -> x0, waiting for transfers between devices: 178 us -> none  [the longest x1 97.8 us: shards(): lax.psum_scatter(partial_sum, 'outer', scatter_dimension=1, tiled=True)]
    psum x1 -> x0, blocking collectives: 79 us -> none  [shards(): lax.psum(jnp.sum(grad_values.astype(jnp.float32), axis=0) * scale, ('oute...]
    pallas_call x0 -> x1, Pallas kernels: none -> 67.8 us  [shards(): pl.pallas_call(functools.partial(kernel, scale), out_shape=(jax.ShapeDtyp...]
    all_gather x1 -> x0, blocking collectives: 40.5 us -> none  [shards(): lax.all_gather(weight, 'outer', axis=0, tiled=True)]
    dot_general x3 -> x0, matrix products: 25.1 us -> none  [the longest x1 13.5 us: shards(): jnp.einsum('toir,th->iorh', tokens_four, grad_values, preferred_element_t...]
    convert_element_type x1 -> x0, local copies, waits for them, and re-layouts: 4.18 us -> none  [shards(): grad_tokens = grad_full.astype(jnp.bfloat16)]
    unnamed x9 -> x8, local copies, waits for them, and re-layouts: 9.04 us -> 9.11 us
  transfers between devices with their start and end apart: 3 -> 0, of which waited for: 2 -> 0; matrix products, arithmetic and copies ran while one was open for 5% -> 0% of each run, Pallas kernels for 0% -> 0%
where the time goes in v1:
time: 78.6 us; the launch traced here: 77.6 us
  Pallas kernels  67.8 us (86%)
  local copies, waits for them, and re-layouts  9.11 us (12%)
    pallas_call x1, Pallas kernels, shards(): pl.pallas_call(functools.partial(kernel, scale), out_shape=(jax.ShapeDtyp...  67.8 us
    unnamed x8, local copies, waits for them, and re-layouts  9.11 us

profile of v1, /device:TPU:8, one launch (start us, length us, event | category | flops | bytes accessed | tf_op | source)
XLA Modules:
  0.0 77.6 jit_solution(16583501597680937757)
XLA Ops:
  0.6 67.8 %shard_map.75 = (bf16[704,512]{1,0:T(8,128)(2,1)}, bf16[704,4096]{1,0:T(8,128)(2,1)}, f32[16,512]{1,0:T(8,128)}, f32[1,512]{1,0:T(1,128)}) custom-call(bf16[704,4096]{1,0:T(8,128)(2,1)} %tok_hbm.1, bf16[16,512]{1,0:T(8,128)(2,1)} %w_hbm.1, f32[1,512]{1,0:T(1,128)} %bitcast.3, bf16[704,512]{1,0:T(8,128)(2,1)} %gv_hbm.1), custom_call_target="tpu_custom_call" | custom-call | flops 8858370048 | bytes 11534336 | tf_op jit(solution)/shard_map/pallas_call | solution.py:466
  68.5 2.0 %copy.12 = bf16[704,512]{1,0:T(8,128)(2,1)} copy(bf16[704,512]{1,0:T(8,128)(2,1)} %get-tuple-element.16) | data formatting | bytes 1441792
  70.5 0.0 copy-start
  70.5 0.0 copy-start.1
  70.5 5.9 %copy.13 = bf16[704,4096]{1,0:T(8,128)(2,1)} copy(bf16[704,4096]{1,0:T(8,128)(2,1)} %get-tuple-element.17) | data formatting | bytes 11534336
  76.4 0.0 copy-done
  76.4 0.6 copy.14
  77.0 0.0 copy-done.1
  77.0 0.6 copy.15
Async XLA Ops:
  70.5 5.9 %copy-start = (f32[16,512]{1,0:T(8,128)S(1)}, f32[16,512]{1,0:T(8,128)}, u32[]{:S(2)}) copy-start(f32[16,512]{1,0:T(8,128)} %get-tuple-element.18) | copy-start | bytes 98308
  70.5 6.5 %copy-start.1 = (f32[1,512]{1,0:T(1,128)S(1)}, f32[1,512]{1,0:T(1,128)}, u32[]{:S(2)}) copy-start(f32[1,512]{1,0:T(1,128)} %get-tuple-element.11) | copy-start | bytes 6148

commit v2 on v0

v2 whole, which is shorter than its diff:
```python
import functools

import jax
import jax.numpy as jnp
from jax import lax
from jax.experimental import pallas as pl
from jax.experimental.pallas import tpu as pltpu
from jax.sharding import PartitionSpec as P

X, Y, Z = 4, 4, 8
MESH = pl.DeviceIdType.MESH
F32, BF16 = jnp.float32, jnp.bfloat16
N_SEM = 240
A_PARTS = ((pl.ds(0, 6), pl.ds(0, 2)), (pl.ds(6, 2), pl.ds(0, 1)))
B_PARTS = (
    (pl.ds(0, 4), pl.ds(2, 1), pl.ds(1, 1)),
    (pl.ds(4, 2), pl.ds(2, 2), pl.ds(1, 2)),
    (pl.ds(6, 2), pl.ds(1, 3), pl.ds(0, 3)),
)
C_PLACES = pl.ds(0, 4)
G3 = pl.ds(3, 1)


def reversed_bits(i):
    return lax.rem(i, 2) * 4 + lax.rem(i // 2, 2) * 2 + i // 4


def kernel(
    scale,
    tok_hbm, w_hbm, bias_ref, gv_hbm,
    valo, gto, gw_ref, gb_ref,
    tok, gv, wb, gall, gr, acc,
    rx1, ry1, rz1, sa, sb, sc, ry2, rx2, rc2, s2, sc2, rz3, rc3,
    bb, bx, by, bz,
    ssem, rsem, dsem, drsem, lsem,
):
    outer = lax.axis_index("outer")
    inner = lax.axis_index("inner")
    c = lax.rem(outer, 2)
    z = lax.rem(outer // 2, Z)
    yl = outer // (2 * Z)
    x = lax.rem(inner, X)
    yh = inner // X
    y = yh * 2 + yl
    pz = reversed_bits(z)
    even = lax.rem(z, 2) == 0
    odd = lax.rem(z, 2) == 1

    def dev(px, py, pz_, pc):
        return {
            "outer": (lax.rem(py, 2) * Z + pz_) * 2 + pc,
            "inner": (py // 2) * X + px,
        }

    def at_x(k):
        p = lax.rem(x + k + X, X)
        return p, dev(p, y, z, c)

    def at_y(k):
        p = lax.rem(y + k + Y, Y)
        return p, dev(x, p, z, c)

    def at_z(k):
        p = lax.rem(z + k + Z, Z)
        return p, dev(x, y, p, c)

    def away(k):
        return (even, odd) if k % 2 == 0 else (odd, even)

    sibling = dev(x, y, z, 1 - c)
    yhl = lambda p: (p // 2, lax.rem(p, 2))
    count = [0]
    sends = []

    def only(when, act):
        if when is None:
            act()
        else:
            pl.when(when)(act)

    def send(src, dst, to, when=None):
        i = count[0]
        count[0] += 1
        cp_ = pltpu.make_async_remote_copy(
            src_ref=src, dst_ref=dst, send_sem=ssem.at[i], recv_sem=rsem.at[i],
            device_id=to, device_id_type=MESH,
        )
        only(when, lambda: cp_.start())
        sends.append((cp_, when))
        return i

    def got(i, dst, when=None):
        cp_ = pltpu.make_async_remote_copy(
            src_ref=dst, dst_ref=dst, send_sem=ssem.at[i], recv_sem=rsem.at[i],
            device_id=sibling, device_id_type=MESH,
        )
        only(when, lambda: cp_.wait_recv())

    half = (1 - yl, yl)
    tok_in = []
    for h in range(2):
        cols = pl.ds(pl.multiple_of(half[h] * 2048, 2048), 2048)
        tok_in.append(pltpu.make_async_copy(tok_hbm.at[:, cols], tok.at[:, cols], lsem.at[h]))
    gv_in = pltpu.make_async_copy(gv_hbm, gv, lsem.at[2])
    w_in = [
        pltpu.make_async_copy(
            w_hbm.at[:, pl.ds(g * 128, 128)], wb.at[yl, pz, c, yh, x, g], lsem.at[3 + g]
        )
        for g in range(4)
    ]
    barrier = pltpu.get_barrier_semaphore()
    peers = [at_z(k)[1] for k in range(1, Z)] + [at_x(k)[1] for k in range(1, X)]
    peers += [at_y(k)[1] for k in range(1, Y)] + [sibling]
    for p in peers:
        pl.semaphore_signal(barrier, inc=1, device_id=p, device_id_type=MESH)
    gv_in.start()
    tok_in[0].start()
    for cp_ in w_in:
        cp_.start()
    tok_in[1].start()

    def d2d(h, i):
        return pltpu.make_async_remote_copy(
            src_ref=gall.at[1 - c, half[h], i], dst_ref=gr.at[half[h], i],
            send_sem=dsem.at[h * Z + i], recv_sem=drsem.at[h * Z + i],
            device_id=sibling, device_id_type=MESH,
        )

    def grads(h, lo, hi, and_send):
        @pl.loop(lo, hi)
        def _(i):
            col = pl.multiple_of((half[h] * Z + reversed_bits(i)) * 256, 256)
            part = lax.dot_general(
                tok[:, pl.ds(col, 256)], gv[...], (((0,), (0,)), ((), ())),
                preferred_element_type=F32,
            ) * scale
            for g in range(4):
                gall[:, half[h], i, :, :, g] = part[:, g * 128:(g + 1) * 128].reshape(
                    2, 2, X, 16, 128
                )
            if and_send:
                d2d(h, i).start()

    gv_in.wait()
    tok_in[0].wait()
    grads(0, 0, 4, False)
    for cp_ in w_in:
        cp_.wait()
    pl.semaphore_wait(barrier, len(peers))

    own = lambda gs: wb.at[yl, pz, c, yh, x, gs]
    ag1, ag1o, agc1 = {}, {}, {}
    for k in range(1, Z):
        to = at_z(k)[1]
        ag1[k] = send(own(pl.ds(0, 3)), own(pl.ds(0, 3)), to)
        ag1o[k] = send(own(G3), own(G3), to, odd)
    for k in range(1, Y):
        agc1[k] = send(own(G3), own(G3), at_y(k)[1], even)

    @pl.loop(0, 4)
    def _(i):
        d2d(0, i).start()

    grads(0, 4, Z, True)

    def combine(h):
        @pl.loop(0, Z)
        def _(i):
            pltpu.make_async_remote_copy(
                src_ref=gr.at[half[h], i], dst_ref=gr.at[half[h], i],
                send_sem=dsem.at[h * Z + i], recv_sem=drsem.at[h * Z + i],
                device_id=sibling, device_id_type=MESH,
            ).wait_recv()
            gall[c, half[h], i] = gall[c, half[h], i] + gr[half[h], i]

    rsa, rsb, rsz = {}, {}, {}

    def scatter_first(h):
        for k in range(1, X):
            p, to = at_x(k)
            for q, (zs, gs) in enumerate(A_PARTS):
                rsa[k, q, h] = send(
                    gall.at[c, half[h], zs, :, p, gs], rx1.at[x, half[h], zs, :, gs], to
                )
        for k in ((1, 3), (2,))[h]:
            p, to = at_y(k)
            for q, (zs, gs, ls) in enumerate(B_PARTS):
                rsb[k, q] = send(
                    gall.at[c, half[h], zs, yhl(p)[0], :, gs], ry1.at[y, zs, :, ls], to
                )
        for k in range(1, Z):
            p, to = at_z(k)
            rsz[k, h] = send(
                gall.at[c, half[h], reversed_bits(p), :, :, G3], rz1.at[z, half[h]], to, away(k)[0]
            )

    combine(0)
    scatter_first(0)

    for k in range(1, Z):
        place = reversed_bits(at_z(-k)[0])
        got(ag1[k], wb.at[yl, place, c, yh, x, pl.ds(0, 3)])
        got(ag1o[k], wb.at[yl, place, c, yh, x, G3], away(k)[1])
    a_piece = lambda py, px, q: wb.at[
        yhl(py)[1], A_PARTS[q][0], c, yhl(py)[0], px, A_PARTS[q][1]
    ]
    b_piece = lambda py, px, q: wb.at[
        yhl(py)[1], B_PARTS[q][0], c, yhl(py)[0], px, B_PARTS[q][1]
    ]
    ag2a, ag2b, agc2, ag3a, ag3b, ag3c = {}, {}, {}, {}, {}, {}
    for k in range(1, Y):
        for q in range(2):
            ref = a_piece(y, x, q)
            ag2a[k, q] = send(ref, ref, at_y(k)[1])
    for k in range(1, X):
        for q in range(3):
            ref = b_piece(y, x, q)
            ag2b[k, q] = send(ref, ref, at_x(k)[1])
    for k in range(1, Y):
        ph, pw = yhl(at_y(-k)[0])
        got(agc1[k], wb.at[pw, pz, c, ph, x, G3], even)
    for k in range(1, X):
        ref = wb.at[:, pz, c, :, x, G3]
        agc2[k] = send(ref, ref, at_x(k)[1], even)

    def spread_a(m):
        for k in range(1, X):
            for q in range(2):
                ref = a_piece(at_y(-m)[0], x, q)
                ag3a[k, q, m] = send(ref, ref, at_x(k)[1])

    def spread_b(m):
        for k in range(1, Y):
            for q in range(3):
                ref = b_piece(y, at_x(-m)[0], q)
                ag3b[k, q, m] = send(ref, ref, at_y(k)[1])

    spread_a(0)
    spread_b(0)

    tok_in[1].wait()
    grads(1, 0, Z, True)
    gvf = gv[...].astype(F32)
    bb[c] = jnp.sum(gvf.reshape(-1, 8, 512), axis=0)
    bias_core = send(bb.at[c], bb.at[c], sibling)

    for m in range(1, X):
        for q in range(2):
            got(ag2a[m, q], a_piece(at_y(-m)[0], x, q))
        spread_a(m)
        for q in range(3):
            got(ag2b[m, q], b_piece(y, at_x(-m)[0], q))
        spread_b(m)
    for k in range(1, X):
        got(agc2[k], wb.at[:, pz, c, :, at_x(-k)[0], G3], even)
    c_slab = lambda p: wb.at[:, reversed_bits(p), c, :, :, G3]
    for k in range(1, Z):
        ag3c[k] = send(c_slab(z), c_slab(z), at_z(k)[1], even)

    combine(1)
    scatter_first(1)

    got(bias_core, bb.at[1 - c])
    bx[x] = bb[0] + bb[1]
    bias_x = [send(bx.at[x], bx.at[x], at_x(k)[1]) for k in range(1, X)]

    a_slab = lambda p, q, cc: wb.at[:, A_PARTS[q][0], cc, :, p, A_PARTS[q][1]]
    b_slab = lambda p, q, cc: wb.at[yhl(p)[1], B_PARTS[q][0], cc, yhl(p)[0], :, B_PARTS[q][1]]
    relay_a, relay_b = {}, {}

    def relay(ref):
        return send(ref, ref, sibling)

    for q in range(2):
        relay_a[0, q] = relay(a_slab(x, q, c))
    for q in range(3):
        relay_b[0, q] = relay(b_slab(y, q, c))
    for k in range(1, X):
        for q in range(2):
            for m in range(Y):
                got(ag3a[k, q, m], a_piece(at_y(-m)[0], at_x(-k)[0], q))
            relay_a[k, q] = relay(a_slab(at_x(-k)[0], q, c))
        for q in range(3):
            for m in range(X):
                got(ag3b[k, q, m], b_piece(at_y(-k)[0], at_x(-m)[0], q))
            relay_b[k, q] = relay(b_slab(at_y(-k)[0], q, c))
    for k in range(1, Z):
        got(ag3c[k], c_slab(at_z(-k)[0]), away(k)[0])
    c_all = lambda cc: wb.at[:, C_PLACES, cc, :, :, G3]
    relay_c = relay(c_all(c))

    for k in range(1, X):
        got(bias_x[k - 1], bx.at[at_x(-k)[0]])
    by[y] = (bx[0] + bx[1]) + (bx[2] + bx[3])
    bias_y = [send(by.at[y], by.at[y], at_y(k)[1]) for k in range(1, Y)]

    rs2a, rs2b, rsc2 = {}, {}, {}

    def second_a(h):
        for q, (zs, gs) in enumerate(A_PARTS):
            total = gall[c, half[h], zs, :, x, gs]
            for k in range(1, X):
                src = at_x(-k)[0]
                got(rsa[k, q, h], rx1.at[src, half[h], zs, :, gs])
                total = total + rx1[src, half[h], zs, :, gs]
            sa[half[h], zs, :, gs] = total
        for k in ((1, 3), (2,))[h]:
            p, to = at_y(k)
            for q, (zs, gs) in enumerate(A_PARTS):
                rs2a[k, q] = send(sa.at[half[h], zs, yhl(p)[0], gs], ry2.at[y, zs, gs], to)

    second_a(0)

    for k in range(X):
        for q in range(2):
            got(relay_a[k, q], a_slab(at_x(-k)[0], q, 1 - c))
        for q in range(3):
            got(relay_b[k, q], b_slab(at_y(-k)[0], q, 1 - c))
    got(relay_c, c_all(1 - c))
    acc[...] = jnp.broadcast_to(bias_ref[...], acc.shape)

    def products(lo, hi):
        @pl.loop(lo, hi)
        def _(j):
            q = lax.rem(j, 4)
            p = lax.rem(q, 2) * 2 + q // 2
            w = jnp.concatenate(
                [
                    jnp.concatenate(
                        [wb[j // 4, p + d, :, :, :, g].reshape(256, 128) for d in (0, 4)], axis=0
                    )
                    for g in range(4)
                ],
                axis=1,
            )
            cols = pl.ds(pl.multiple_of(j * 512, 512), 512)
            gto[:, cols] = lax.dot_general(
                gv[...], w, (((1,), (1,)), ((), ())), preferred_element_type=F32
            ).astype(BF16)
            acc[...] += jnp.dot(tok[:, cols], w, preferred_element_type=F32)

    products(0, 6)

    second_a(1)
    for q, (zs, gs, ls) in enumerate(B_PARTS):
        total = gall[c, yl, zs, yh, :, gs]
        for k in range(1, Y):
            src = at_y(-k)[0]
            got(rsb[k, q], ry1.at[src, zs, :, ls])
            total = total + ry1[src, zs, :, ls]
        sb[zs, :, ls] = total
    for k in range(1, X):
        p, to = at_x(k)
        for q, (zs, gs, ls) in enumerate(B_PARTS):
            rs2b[k, q] = send(sb.at[zs, p, ls], rx2.at[x, zs, ls], to)
    for k in range(1, Z):
        for h in range(2):
            got(rsz[k, h], rz1.at[at_z(-k)[0], half[h]], even)

    @pl.when(even)
    def _():
        total = gall[c, :, pz, :, :, G3]
        for k in range(1, Z):
            total = total + rz1[at_z(-k)[0]]
        sc[...] = total

    for k in range(1, X):
        p, to = at_x(k)
        rsc2[k] = send(sc.at[:, :, p], rc2.at[x], to, even)

    for k in range(1, Y):
        got(bias_y[k - 1], by.at[at_y(-k)[0]])
    bz[z] = (by[0] + by[1]) + (by[2] + by[3])
    bias_z = [send(bz.at[z], bz.at[z], at_z(k)[1]) for k in range(1, Z)]
    products(6, 8)

    for q, (zs, gs) in enumerate(A_PARTS):
        total = sa[yl, zs, yh, gs]
        for k in range(1, Y):
            src = at_y(-k)[0]
            got(rs2a[k, q], ry2.at[src, zs, gs])
            total = total + ry2[src, zs, gs]
        s2[zs, gs] = total
    for q, (zs, gs, ls) in enumerate(B_PARTS):
        total = sb[zs, x, ls]
        for k in range(1, X):
            src = at_x(-k)[0]
            got(rs2b[k, q], rx2.at[src, zs, ls])
            total = total + rx2[src, zs, ls]
        s2[zs, gs] = total
    rs3, rs3o, rsc3 = {}, {}, {}
    first3 = pl.ds(0, 3)
    for k in range(1, Z):
        p, to = at_z(k)
        place = reversed_bits(p)
        rs3[k] = send(s2.at[place, first3], rz3.at[z, first3], to)
        rs3o[k] = send(s2.at[place, G3], rz3.at[z, G3], to, away(k)[1])
    for k in range(1, X):
        got(rsc2[k], rc2.at[at_x(-k)[0]], even)

    @pl.when(even)
    def _():
        total = sc[:, :, x]
        for k in range(1, X):
            total = total + rc2[at_x(-k)[0]]
        sc2[...] = total

    for k in range(1, Y):
        p, to = at_y(k)
        ph, pw = yhl(p)
        rsc3[k] = send(sc2.at[pw, ph], rc3.at[y], to, even)
    valo[...] = acc[...].astype(BF16)

    for k in range(1, Z):
        got(bias_z[k - 1], bz.at[at_z(-k)[0]])
    total = bz[0]
    for k in range(1, Z):
        total = total + bz[k]
    gb_ref[...] = jnp.sum(total, axis=0, keepdims=True) * scale
    for k in range(1, Y):
        got(rsc3[k], rc3.at[at_y(-k)[0]], even)

    @pl.when(even)
    def _():
        total = sc2[yl, yh, 0]
        for k in range(1, Y):
            total = total + rc3[at_y(-k)[0], 0]
        gw_ref[:, pl.ds(384, 128)] = total

    for k in range(1, Z):
        got(rs3[k], rz3.at[at_z(-k)[0], first3])
        got(rs3o[k], rz3.at[at_z(-k)[0], G3], odd)
    total = s2[pz, first3]
    for k in range(1, Z):
        total = total + rz3[at_z(-k)[0], first3]
    for g in range(3):
        gw_ref[:, pl.ds(g * 128, 128)] = total[g]

    @pl.when(odd)
    def _():
        total = s2[pz, 3]
        for k in range(1, Z):
            total = total + rz3[at_z(-k)[0], 3]
        gw_ref[:, pl.ds(384, 128)] = total

    for cp_, when in sends:
        only(when, lambda: cp_.wait_send())

    @pl.loop(0, 2 * Z)
    def _(i):
        pltpu.make_async_remote_copy(
            src_ref=gr.at[0, 0], dst_ref=gr.at[0, 0], send_sem=dsem.at[i], recv_sem=drsem.at[i],
            device_id=sibling, device_id_type=MESH,
        ).wait_send()
    assert count[0] <= N_SEM, count[0]


def write_kernel(val, gt, gw, gb, val_out, gt_out, gw_out, gb_out, sem):
    copies = [pltpu.make_async_copy(val, val_out, sem.at[0])]
    rows = gt.shape[0] // 4
    for q in range(4):
        part = pl.ds(q * rows, rows)
        copies.append(pltpu.make_async_copy(gt.at[part], gt_out.at[part], sem.at[1 + q]))
    copies.append(pltpu.make_async_copy(gw, gw_out, sem.at[5]))
    copies.append(pltpu.make_async_copy(gb, gb_out, sem.at[6]))
    for cp_ in copies:
        cp_.start()
    for cp_ in copies:
        cp_.wait()


def shards(tokens, weight, bias, grad_values):
    rows, width = tokens.shape
    feats = weight.shape[1]
    n = lax.axis_size("outer") * lax.axis_size("inner")
    scale = float(1.0 / (rows * n) ** 0.5)
    anyspace = pl.BlockSpec(memory_space=pl.ANY)
    vmem = pl.BlockSpec(memory_space=pltpu.VMEM)
    tile = (16, 128)
    scratch = [
        ((rows, width), BF16),
        ((rows, feats), BF16),
        ((2, Z, 2, 2, X, 4) + tile, BF16),
        ((2, 2, Z, 2, X, 4) + tile, F32),
        ((2, Z, 2, X, 4) + tile, F32),
        ((rows, feats), F32),
        ((X, 2, Z, 2, 2) + tile, F32),
        ((Y, Z, X, 3) + tile, F32),
        ((Z, 2, 2, X, 1) + tile, F32),
        ((2, Z, 2, 2) + tile, F32),
        ((Z, X, 3) + tile, F32),
        ((2, 2, X, 1) + tile, F32),
        ((Y, Z, 2) + tile, F32),
        ((X, Z, 3) + tile, F32),
        ((X, 2, 2, 1) + tile, F32),
        ((Z, 4) + tile, F32),
        ((2, 2, 1) + tile, F32),
        ((Z, 4) + tile, F32),
        ((Y, 1) + tile, F32),
        ((2, 8, feats), F32),
        ((X, 8, feats), F32),
        ((Y, 8, feats), F32),
        ((Z, 8, feats), F32),
    ]
    dma = pltpu.SemaphoreType.DMA
    outs = (
        ((rows, feats), BF16),
        ((rows, width), BF16),
        (weight.shape, F32),
        ((1, feats), F32),
    )
    results = pl.pallas_call(
        functools.partial(kernel, scale),
        out_shape=tuple(pltpu.VMEM(s, d) for s, d in outs),
        in_specs=[anyspace, anyspace, vmem, anyspace],
        out_specs=(vmem,) * 4,
        scratch_shapes=[pltpu.VMEM(s, d) for s, d in scratch]
        + [dma((N_SEM,)), dma((N_SEM,)), dma((2 * Z,)), dma((2 * Z,)), dma((8,))],
        compiler_params=pltpu.CompilerParams(
            collective_id=0, has_side_effects=True, vmem_limit_bytes=50 * 1024 * 1024
        ),
        cost_estimate=pl.CostEstimate(
            flops=6 * rows * width * feats, bytes_accessed=4 * rows * width, transcendentals=0
        ),
        name="gather_scatter",
    )(tokens, weight, bias.reshape(1, feats), grad_values)
    values, grad_tokens, grad_weight, grad_bias = pl.pallas_call(
        write_kernel,
        out_shape=tuple(jax.ShapeDtypeStruct(s, d) for s, d in outs),
        in_specs=[vmem] * 4,
        out_specs=(anyspace,) * 4,
        scratch_shapes=[dma((8,))],
        compiler_params=pltpu.CompilerParams(vmem_limit_bytes=1024 * 1024),
        name="write",
    )(*[pltpu.with_memory_space_constraint(r, pltpu.VMEM) for r in results])
    return values, grad_tokens, grad_weight, grad_bias.reshape(feats)


def solution(mesh):
    in_specs = (
        P(("outer", "inner"), None),
        P(("outer", "inner"), None),
        P(),
        P(("outer", "inner"), None),
    )
    out_specs = (
        P(("outer", "inner"), None),
        P(("outer", "inner"), None),
        P(("outer", "inner"), None),
        P(),
    )
    return jax.shard_map(shards, mesh=mesh, in_specs=in_specs, out_specs=out_specs, check_vma=False)
```

time: 355 us -> 79.9 us (0.23)
  waiting for transfers between devices: 178 us -> 0 us
  blocking collectives: 120 us -> 0 us
  Pallas kernels: 0 us -> 79.1 us
  matrix products: 25.1 us -> 0 us
  local copies, waits for them, and re-layouts: 16 us -> 0 us
  between operations: 13.8 us -> 0.64 us
    reduce_scatter x2 -> x0, waiting for transfers between devices: 178 us -> none  [the longest x1 97.8 us: shards(): lax.psum_scatter(partial_sum, 'outer', scatter_dimension=1, tiled=True)]
    pallas_call x0 -> x2, Pallas kernels: none -> 79.1 us  [the longest x1 76.3 us: shards(): pl.pallas_call(functools.partial(kernel, scale), out_shape=tuple((pltpu.V...]
    psum x1 -> x0, blocking collectives: 79 us -> none  [shards(): lax.psum(jnp.sum(grad_values.astype(jnp.float32), axis=0) * scale, ('oute...]
    all_gather x1 -> x0, blocking collectives: 40.5 us -> none  [shards(): lax.all_gather(weight, 'outer', axis=0, tiled=True)]
    dot_general x3 -> x0, matrix products: 25.1 us -> none  [the longest x1 13.5 us: shards(): jnp.einsum('toir,th->iorh', tokens_four, grad_values, preferred_element_t...]
    unnamed x9 -> x0, local copies, waits for them, and re-layouts: 9.04 us -> none
    convert_element_type x1 -> x0, local copies, waits for them, and re-layouts: 4.18 us -> none  [shards(): grad_tokens = grad_full.astype(jnp.bfloat16)]
  transfers between devices with their start and end apart: 3 -> 0, of which waited for: 2 -> 0; matrix products, arithmetic and copies ran while one was open for 5% -> 0% of each run, Pallas kernels for 0% -> 0%
where the time goes in v2:
time: 79.9 us; the launch traced here: 79.8 us
  Pallas kernels  79.1 us (99%)
    pallas_call x1, Pallas kernels, shards(): pl.pallas_call(functools.partial(kernel, scale), out_shape=tuple((pltpu.V...  76.3 us
    pallas_call x1, Pallas kernels, shards(): pl.pallas_call(write_kernel, out_shape=tuple((jax.ShapeDtypeStruct(s, d)...  2.84 us

profile of v2, /device:TPU:8, one launch (start us, length us, event | category | flops | bytes accessed | tf_op | source)
XLA Modules:
  0.0 79.8 jit_solution(2419858477219699227)
XLA Ops:
  0.6 76.3 %gather_scatter.1 = (bf16[704,512]{1,0:T(8,128)(2,1)S(1)}, bf16[704,4096]{1,0:T(8,128)(2,1)S(1)}, f32[16,512]{1,0:T(8,128)S(1)}, f32[1,512]{1,0:T(1,128)S(1)}) custom-call(bf16[704,4096]{1,0:T(8,128)(2,1)} %tok_hbm.1, bf16[16,512]{1,0:T(8,128)(2,1)} %w_hbm.1, f32[1,512]{1,0:T(1,128)} %bitcast.2, bf16[704,512]{1,0:T(8,128)(2,1)} %gv_hbm.1), custom_call_target="tpu_custom_call" | custom-call | flops 8858370048 | bytes 11534336 | tf_op jit(solution)/shard_map/gather_scatter/pallas_call | solution.py:512
  76.9 2.8 %write.1 = (bf16[704,512]{1,0:T(8,128)(2,1)}, bf16[704,4096]{1,0:T(8,128)(2,1)}, f32[16,512]{1,0:T(8,128)}, f32[1,512]{1,0:T(1,128)}) custom-call(bf16[704,512]{1,0:T(8,128)(2,1)S(1)} %get-tuple-element.12.val, bf16[704,4096]{1,0:T(8,128)(2,1)S(1)} %get-tuple-element.13.gt, f32[16,512]{1,0:T(8,128)S(1)} %get-tuple-element.14.gw, ...), custom_call_target="tpu_custom_call" | custom-call | tf_op jit(solution)/shard_map/write/pallas_call | solution.py:527

commit v3 on v2

--- a/solution.py
+++ b/solution.py
@@ -10,7 +10,7 @@
 X, Y, Z = 4, 4, 8
 MESH = pl.DeviceIdType.MESH
 F32, BF16 = jnp.float32, jnp.bfloat16
-N_SEM = 240
+N_SEM = 260
 A_PARTS = ((pl.ds(0, 6), pl.ds(0, 2)), (pl.ds(6, 2), pl.ds(0, 1)))
 B_PARTS = (
     (pl.ds(0, 4), pl.ds(2, 1), pl.ds(1, 1)),
@@ -21,6 +21,35 @@
 G3 = pl.ds(3, 1)
 
 
+TOP = 2.0 ** 15.5
+LEAST = 2.0 ** -100
+NORMAL = 2.0 ** -126
+
+
+def tiles(v):
+    return v.reshape(v.shape[:-2] + (2, 8, 128))
+
+
+def largest(v):
+    return jnp.max(jnp.abs(v).reshape(-1, 8, 128), axis=0)
+
+
+def encode(v, inverse):
+    r = (tiles(v) * inverse).reshape(v.shape)
+    r2 = r * r
+    r4 = r2 * r2
+    r8 = r4 * r4
+    return jnp.where(r < 0, -r8, r8).astype(BF16)
+
+
+def decode(code, unit):
+    v = code.astype(F32)
+    r2 = lax.rsqrt(jnp.maximum(jnp.abs(v), NORMAL))
+    r4 = lax.rsqrt(r2)
+    root = r4 * lax.rsqrt(r4)
+    return (tiles(jnp.where(v < 0, -root, root)) * unit).reshape(v.shape)
+
+
 def reversed_bits(i):
     return lax.rem(i, 2) * 4 + lax.rem(i // 2, 2) * 2 + i // 4
 
@@ -31,6 +60,7 @@
     valo, gto, gw_ref, gb_ref,
     tok, gv, wb, gall, gr, acc,
     rx1, ry1, rz1, sa, sb, sc, ry2, rx2, rc2, s2, sc2, rz3, rc3,
+    code, ea, eb, u, ux, uy, uz, u2, u2y, u2x,
     bb, bx, by, bz,
     ssem, rsem, dsem, drsem, lsem,
 ):
@@ -164,35 +194,47 @@
     grads(0, 4, Z, True)
 
     def combine(h):
-        @pl.loop(0, Z)
-        def _(i):
+        def add(i, top):
             pltpu.make_async_remote_copy(
                 src_ref=gr.at[half[h], i], dst_ref=gr.at[half[h], i],
                 send_sem=dsem.at[h * Z + i], recv_sem=drsem.at[h * Z + i],
                 device_id=sibling, device_id_type=MESH,
             ).wait_recv()
-            gall[c, half[h], i] = gall[c, half[h], i] + gr[half[h], i]
-
-    rsa, rsb, rsz = {}, {}, {}
+            both = gall[c, half[h], i] + gr[half[h], i]
+            gall[c, half[h], i] = both
+            return jnp.maximum(top, largest(both))
+
+        top = lax.fori_loop(0, Z, add, jnp.full((8, 128), LEAST, F32))
+        u[h] = top * (1.0 / TOP)
+        inverse = TOP / top
+
+        @pl.loop(0, Z)
+        def _(i):
+            code[half[h], i] = encode(gall[c, half[h], i], inverse)
+
+    rsa, rsb, rsz, rsu = {}, {}, {}, {}
 
     def scatter_first(h):
         for k in range(1, X):
             p, to = at_x(k)
             for q, (zs, gs) in enumerate(A_PARTS):
                 rsa[k, q, h] = send(
-                    gall.at[c, half[h], zs, :, p, gs], rx1.at[x, half[h], zs, :, gs], to
+                    code.at[half[h], zs, :, p, gs], rx1.at[x, half[h], zs, :, gs], to
                 )
+            rsu["x", k, h] = send(u.at[h], ux.at[x, h], to)
         for k in ((1, 3), (2,))[h]:
             p, to = at_y(k)
             for q, (zs, gs, ls) in enumerate(B_PARTS):
                 rsb[k, q] = send(
-                    gall.at[c, half[h], zs, yhl(p)[0], :, gs], ry1.at[y, zs, :, ls], to
+                    code.at[half[h], zs, yhl(p)[0], :, gs], ry1.at[y, zs, :, ls], to
                 )
+            rsu["y", k] = send(u.at[h], uy.at[y], to)
         for k in range(1, Z):
             p, to = at_z(k)
             rsz[k, h] = send(
-                gall.at[c, half[h], reversed_bits(p), :, :, G3], rz1.at[z, half[h]], to, away(k)[0]
+                code.at[half[h], reversed_bits(p), :, :, G3], rz1.at[z, half[h]], to, away(k)[0]
             )
+            rsu["z", k, h] = send(u.at[h], uz.at[z, half[h]], to, away(k)[0])
 
     combine(0)
     scatter_first(0)
@@ -244,6 +286,9 @@
     bb[c] = jnp.sum(gvf.reshape(-1, 8, 512), axis=0)
     bias_core = send(bb.at[c], bb.at[c], sibling)
 
+    combine(1)
+    scatter_first(1)
+
     for m in range(1, X):
         for q in range(2):
             got(ag2a[m, q], a_piece(at_y(-m)[0], x, q))
@@ -257,12 +302,71 @@
     for k in range(1, Z):
         ag3c[k] = send(c_slab(z), c_slab(z), at_z(k)[1], even)
 
-    combine(1)
-    scatter_first(1)
-
     got(bias_core, bb.at[1 - c])
     bx[x] = bb[0] + bb[1]
     bias_x = [send(bx.at[x], bx.at[x], at_x(k)[1]) for k in range(1, X)]
+
+    rs2a, rs2b, rsc2 = {}, {}, {}
+
+    def second_a(h):
+        top = jnp.full((8, 128), LEAST, F32)
+        for k in range(1, X):
+            got(rsu["x", k, h], ux.at[at_x(-k)[0], h])
+        for q, (zs, gs) in enumerate(A_PARTS):
+            total = gall[c, half[h], zs, :, x, gs]
+            for k in range(1, X):
+                src = at_x(-k)[0]
+                got(rsa[k, q, h], rx1.at[src, half[h], zs, :, gs])
+                total = total + decode(rx1[src, half[h], zs, :, gs], ux[src, h])
+            sa[half[h], zs, :, gs] = total
+            top = jnp.maximum(top, largest(total))
+        u2[h] = top * (1.0 / TOP)
+        for zs, gs in A_PARTS:
+            ea[half[h], zs, :, gs] = encode(sa[half[h], zs, :, gs], TOP / top)
+        for k in ((1, 3), (2,))[h]:
+            p, to = at_y(k)
+            for q, (zs, gs) in enumerate(A_PARTS):
+                rs2a[k, q] = send(ea.at[half[h], zs, yhl(p)[0], gs], ry2.at[y, zs, gs], to)
+            rsu["y2", k] = send(u2.at[h], u2y.at[y], to)
+
+    second_a(0)
+    second_a(1)
+    top = jnp.full((8, 128), LEAST, F32)
+    for k in range(1, Y):
+        got(rsu["y", k], uy.at[at_y(-k)[0]])
+    for q, (zs, gs, ls) in enumerate(B_PARTS):
+        total = gall[c, yl, zs, yh, :, gs]
+        for k in range(1, Y):
+            src = at_y(-k)[0]
+            got(rsb[k, q], ry1.at[src, zs, :, ls])
+            total = total + decode(ry1[src, zs, :, ls], uy[src])
+        sb[zs, :, ls] = total
+        top = jnp.maximum(top, largest(total))
+    u2[2] = top * (1.0 / TOP)
+    for zs, gs, ls in B_PARTS:
+        eb[zs, :, ls] = encode(sb[zs, :, ls], TOP / top)
+    for k in range(1, X):
+        p, to = at_x(k)
+        for q, (zs, gs, ls) in enumerate(B_PARTS):
+            rs2b[k, q] = send(eb.at[zs, p, ls], rx2.at[x, zs, ls], to)
+        rsu["x2", k] = send(u2.at[2], u2x.at[x], to)
+    for k in range(1, Z):
+        for h in range(2):
+            got(rsz[k, h], rz1.at[at_z(-k)[0], half[h]], even)
+            got(rsu["z", k, h], uz.at[at_z(-k)[0], half[h]], even)
+
+    @pl.when(even)
+    def _():
+        for w in range(2):
+            total = gall[c, w, pz, :, :, G3]
+            for k in range(1, Z):
+                src = at_z(-k)[0]
+                total = total + decode(rz1[src, w], uz[src, w])
+            sc[w] = total
+
+    for k in range(1, X):
+        p, to = at_x(k)
+        rsc2[k] = send(sc.at[:, :, p], rc2.at[x], to, even)
 
     a_slab = lambda p, q, cc: wb.at[:, A_PARTS[q][0], cc, :, p, A_PARTS[q][1]]
     b_slab = lambda p, q, cc: wb.at[yhl(p)[1], B_PARTS[q][0], cc, yhl(p)[0], :, B_PARTS[q][1]]
@@ -293,23 +397,6 @@
         got(bias_x[k - 1], bx.at[at_x(-k)[0]])
     by[y] = (bx[0] + bx[1]) + (bx[2] + bx[3])
     bias_y = [send(by.at[y], by.at[y], at_y(k)[1]) for k in range(1, Y)]
-
-    rs2a, rs2b, rsc2 = {}, {}, {}
-
-    def second_a(h):
-        for q, (zs, gs) in enumerate(A_PARTS):
-            total = gall[c, half[h], zs, :, x, gs]
-            for k in range(1, X):
-                src = at_x(-k)[0]
-                got(rsa[k, q, h], rx1.at[src, half[h], zs, :, gs])
-                total = total + rx1[src, half[h], zs, :, gs]
-            sa[half[h], zs, :, gs] = total
-        for k in ((1, 3), (2,))[h]:
-            p, to = at_y(k)
-            for q, (zs, gs) in enumerate(A_PARTS):
-                rs2a[k, q] = send(sa.at[half[h], zs, yhl(p)[0], gs], ry2.at[y, zs, gs], to)
-
-    second_a(0)
 
     for k in range(X):
         for q in range(2):
@@ -339,54 +426,29 @@
             ).astype(BF16)
             acc[...] += jnp.dot(tok[:, cols], w, preferred_element_type=F32)
 
-    products(0, 6)
-
-    second_a(1)
-    for q, (zs, gs, ls) in enumerate(B_PARTS):
-        total = gall[c, yl, zs, yh, :, gs]
-        for k in range(1, Y):
-            src = at_y(-k)[0]
-            got(rsb[k, q], ry1.at[src, zs, :, ls])
-            total = total + ry1[src, zs, :, ls]
-        sb[zs, :, ls] = total
-    for k in range(1, X):
-        p, to = at_x(k)
-        for q, (zs, gs, ls) in enumerate(B_PARTS):
-            rs2b[k, q] = send(sb.at[zs, p, ls], rx2.at[x, zs, ls], to)
-    for k in range(1, Z):
-        for h in range(2):
-            got(rsz[k, h], rz1.at[at_z(-k)[0], half[h]], even)
-
-    @pl.when(even)
-    def _():
-        total = gall[c, :, pz, :, :, G3]
-        for k in range(1, Z):
-            total = total + rz1[at_z(-k)[0]]
-        sc[...] = total
-
-    for k in range(1, X):
-        p, to = at_x(k)
-        rsc2[k] = send(sc.at[:, :, p], rc2.at[x], to, even)
+    products(0, 4)
 
     for k in range(1, Y):
         got(bias_y[k - 1], by.at[at_y(-k)[0]])
     bz[z] = (by[0] + by[1]) + (by[2] + by[3])
     bias_z = [send(bz.at[z], bz.at[z], at_z(k)[1]) for k in range(1, Z)]
-    products(6, 8)
-
+    for k in range(1, Y):
+        got(rsu["y2", k], u2y.at[at_y(-k)[0]])
     for q, (zs, gs) in enumerate(A_PARTS):
         total = sa[yl, zs, yh, gs]
         for k in range(1, Y):
             src = at_y(-k)[0]
             got(rs2a[k, q], ry2.at[src, zs, gs])
-            total = total + ry2[src, zs, gs]
+            total = total + decode(ry2[src, zs, gs], u2y[src])
         s2[zs, gs] = total
+    for k in range(1, X):
+        got(rsu["x2", k], u2x.at[at_x(-k)[0]])
     for q, (zs, gs, ls) in enumerate(B_PARTS):
         total = sb[zs, x, ls]
         for k in range(1, X):
             src = at_x(-k)[0]
             got(rs2b[k, q], rx2.at[src, zs, ls])
-            total = total + rx2[src, zs, ls]
+            total = total + decode(rx2[src, zs, ls], u2x[src])
         s2[zs, gs] = total
     rs3, rs3o, rsc3 = {}, {}, {}
     first3 = pl.ds(0, 3)
@@ -409,6 +471,7 @@
         p, to = at_y(k)
         ph, pw = yhl(p)
         rsc3[k] = send(sc2.at[pw, ph], rc3.at[y], to, even)
+    products(4, 8)
     valo[...] = acc[...].astype(BF16)
 
     for k in range(1, Z):
@@ -484,19 +547,29 @@
         ((2, 2, Z, 2, X, 4) + tile, F32),
         ((2, Z, 2, X, 4) + tile, F32),
         ((rows, feats), F32),
-        ((X, 2, Z, 2, 2) + tile, F32),
-        ((Y, Z, X, 3) + tile, F32),
-        ((Z, 2, 2, X, 1) + tile, F32),
+        ((X, 2, Z, 2, 2) + tile, BF16),
+        ((Y, Z, X, 3) + tile, BF16),
+        ((Z, 2, 2, X, 1) + tile, BF16),
         ((2, Z, 2, 2) + tile, F32),
         ((Z, X, 3) + tile, F32),
         ((2, 2, X, 1) + tile, F32),
-        ((Y, Z, 2) + tile, F32),
-        ((X, Z, 3) + tile, F32),
+        ((Y, Z, 2) + tile, BF16),
+        ((X, Z, 3) + tile, BF16),
         ((X, 2, 2, 1) + tile, F32),
         ((Z, 4) + tile, F32),
         ((2, 2, 1) + tile, F32),
         ((Z, 4) + tile, F32),
         ((Y, 1) + tile, F32),
+        ((2, Z, 2, X, 4) + tile, BF16),
+        ((2, Z, 2, 2) + tile, BF16),
+        ((Z, X, 3) + tile, BF16),
+        ((2, 8, 128), F32),
+        ((X, 2, 8, 128), F32),
+        ((Y, 8, 128), F32),
+        ((Z, 2, 8, 128), F32),
+        ((3, 8, 128), F32),
+        ((Y, 8, 128), F32),
+        ((X, 8, 128), F32),
         ((2, 8, feats), F32),
         ((X, 8, feats), F32),
         ((Y, 8, feats), F32),

time: 79.9 us -> 67.7 us (0.85); the launches traced: 79.8 us -> 66.7 us
  Pallas kernels: 79.1 us -> 66.1 us
    pallas_call x1, Pallas kernels: 76.3 us -> 63.3 us  [shards(): pl.pallas_call(functools.partial(kernel, scale), out_shape=tuple((pltpu.V...]
where the time goes in v3:
time: 67.7 us; the launch traced here: 66.7 us
  Pallas kernels  66.1 us (98%)
    pallas_call x1, Pallas kernels, shards(): pl.pallas_call(functools.partial(kernel, scale), out_shape=tuple((pltpu.V...  63.3 us
    pallas_call x1, Pallas kernels, shards(): pl.pallas_call(write_kernel, out_shape=tuple((jax.ShapeDtypeStruct(s, d)...  2.84 us

profile of v3, /device:TPU:8, one launch (start us, length us, event | category | flops | bytes accessed | tf_op | source)
XLA Modules:
  0.0 66.7 jit_solution(1665927635324263216)
XLA Ops:
  0.6 63.3 %gather_scatter.1 = (bf16[704,512]{1,0:T(8,128)(2,1)S(1)}, bf16[704,4096]{1,0:T(8,128)(2,1)S(1)}, f32[16,512]{1,0:T(8,128)S(1)}, f32[1,512]{1,0:T(1,128)S(1)}) custom-call(bf16[704,4096]{1,0:T(8,128)(2,1)} %tok_hbm.1, bf16[16,512]{1,0:T(8,128)(2,1)} %w_hbm.1, f32[1,512]{1,0:T(1,128)} %bitcast.2, bf16[704,512]{1,0:T(8,128)(2,1)} %gv_hbm.1), custom_call_target="tpu_custom_call" | custom-call | flops 8858370048 | bytes 11534336 | tf_op jit(solution)/shard_map/gather_scatter/pallas_call | solution.py:585
  63.9 2.8 %write.1 = (bf16[704,512]{1,0:T(8,128)(2,1)}, bf16[704,4096]{1,0:T(8,128)(2,1)}, f32[16,512]{1,0:T(8,128)}, f32[1,512]{1,0:T(1,128)}) custom-call(bf16[704,512]{1,0:T(8,128)(2,1)S(1)} %get-tuple-element.12.val, bf16[704,4096]{1,0:T(8,128)(2,1)S(1)} %get-tuple-element.13.gt, f32[16,512]{1,0:T(8,128)S(1)} %get-tuple-element.14.gw, ...), custom_call_target="tpu_custom_call" | custom-call | tf_op jit(solution)/shard_map/write/pallas_call | solution.py:600

commit v4 on v3

--- a/solution.py
+++ b/solution.py
@@ -138,6 +138,8 @@
         )
         for g in range(4)
     ]
+    for cp_ in w_in:
+        cp_.start()
     barrier = pltpu.get_barrier_semaphore()
     peers = [at_z(k)[1] for k in range(1, Z)] + [at_x(k)[1] for k in range(1, X)]
     peers += [at_y(k)[1] for k in range(1, Y)] + [sibling]
@@ -145,8 +147,6 @@
         pl.semaphore_signal(barrier, inc=1, device_id=p, device_id_type=MESH)
     gv_in.start()
     tok_in[0].start()
-    for cp_ in w_in:
-        cp_.start()
     tok_in[1].start()
 
     def d2d(h, i):
@@ -156,8 +156,8 @@
             device_id=sibling, device_id_type=MESH,
         )
 
-    def grads(h, lo, hi, and_send):
-        @pl.loop(lo, hi)
+    def grads(h):
+        @pl.loop(0, Z)
         def _(i):
             col = pl.multiple_of((half[h] * Z + reversed_bits(i)) * 256, 256)
             part = lax.dot_general(
@@ -168,12 +168,8 @@
                 gall[:, half[h], i, :, :, g] = part[:, g * 128:(g + 1) * 128].reshape(
                     2, 2, X, 16, 128
                 )
-            if and_send:
-                d2d(h, i).start()
-
-    gv_in.wait()
-    tok_in[0].wait()
-    grads(0, 0, 4, False)
+            d2d(h, i).start()
+
     for cp_ in w_in:
         cp_.wait()
     pl.semaphore_wait(barrier, len(peers))
@@ -187,11 +183,9 @@
     for k in range(1, Y):
         agc1[k] = send(own(G3), own(G3), at_y(k)[1], even)
 
-    @pl.loop(0, 4)
-    def _(i):
-        d2d(0, i).start()
-
-    grads(0, 4, Z, True)
+    gv_in.wait()
+    tok_in[0].wait()
+    grads(0)
 
     def combine(h):
         def add(i, top):
@@ -281,7 +275,7 @@
     spread_b(0)
 
     tok_in[1].wait()
-    grads(1, 0, Z, True)
+    grads(1)
     gvf = gv[...].astype(F32)
     bb[c] = jnp.sum(gvf.reshape(-1, 8, 512), axis=0)
     bias_core = send(bb.at[c], bb.at[c], sibling)
@@ -398,6 +392,45 @@
     by[y] = (bx[0] + bx[1]) + (bx[2] + bx[3])
     bias_y = [send(by.at[y], by.at[y], at_y(k)[1]) for k in range(1, Y)]
 
+    for k in range(1, Y):
+        got(rsu["y2", k], u2y.at[at_y(-k)[0]])
+    for q, (zs, gs) in enumerate(A_PARTS):
+        total = sa[yl, zs, yh, gs]
+        for k in range(1, Y):
+            src = at_y(-k)[0]
+            got(rs2a[k, q], ry2.at[src, zs, gs])
+            total = total + decode(ry2[src, zs, gs], u2y[src])
+        s2[zs, gs] = total
+    for k in range(1, X):
+        got(rsu["x2", k], u2x.at[at_x(-k)[0]])
+    for q, (zs, gs, ls) in enumerate(B_PARTS):
+        total = sb[zs, x, ls]
+        for k in range(1, X):
+            src = at_x(-k)[0]
+            got(rs2b[k, q], rx2.at[src, zs, ls])
+            total = total + decode(rx2[src, zs, ls], u2x[src])
+        s2[zs, gs] = total
+    rs3, rs3o, rsc3 = {}, {}, {}
+    first3 = pl.ds(0, 3)
+    for k in range(1, Z):
+        p, to = at_z(k)
+        place = reversed_bits(p)
+        rs3[k] = send(s2.at[place, first3], rz3.at[z, first3], to)
+        rs3o[k] = send(s2.at[place, G3], rz3.at[z, G3], to, away(k)[1])
+    for k in range(1, X):
+        got(rsc2[k], rc2.at[at_x(-k)[0]], even)
+
+    @pl.when(even)
+    def _():
+        total = sc[:, :, x]
+        for k in range(1, X):
+            total = total + rc2[at_x(-k)[0]]
+        sc2[...] = total
+
+    for k in range(1, Y):
+        p, to = at_y(k)
+        ph, pw = yhl(p)
+        rsc3[k] = send(sc2.at[pw, ph], rc3.at[y], to, even)
     for k in range(X):
         for q in range(2):
             got(relay_a[k, q], a_slab(at_x(-k)[0], q, 1 - c))
@@ -432,45 +465,6 @@
         got(bias_y[k - 1], by.at[at_y(-k)[0]])
     bz[z] = (by[0] + by[1]) + (by[2] + by[3])
     bias_z = [send(bz.at[z], bz.at[z], at_z(k)[1]) for k in range(1, Z)]
-    for k in range(1, Y):
-        got(rsu["y2", k], u2y.at[at_y(-k)[0]])
-    for q, (zs, gs) in enumerate(A_PARTS):
-        total = sa[yl, zs, yh, gs]
-        for k in range(1, Y):
-            src = at_y(-k)[0]
-            got(rs2a[k, q], ry2.at[src, zs, gs])
-            total = total + decode(ry2[src, zs, gs], u2y[src])
-        s2[zs, gs] = total
-    for k in range(1, X):
-        got(rsu["x2", k], u2x.at[at_x(-k)[0]])
-    for q, (zs, gs, ls) in enumerate(B_PARTS):
-        total = sb[zs, x, ls]
-        for k in range(1, X):
-            src = at_x(-k)[0]
-            got(rs2b[k, q], rx2.at[src, zs, ls])
-            total = total + decode(rx2[src, zs, ls], u2x[src])
-        s2[zs, gs] = total
-    rs3, rs3o, rsc3 = {}, {}, {}
-    first3 = pl.ds(0, 3)
-    for k in range(1, Z):
-        p, to = at_z(k)
-        place = reversed_bits(p)
-        rs3[k] = send(s2.at[place, first3], rz3.at[z, first3], to)
-        rs3o[k] = send(s2.at[place, G3], rz3.at[z, G3], to, away(k)[1])
-    for k in range(1, X):
-        got(rsc2[k], rc2.at[at_x(-k)[0]], even)
-
-    @pl.when(even)
-    def _():
-        total = sc[:, :, x]
-        for k in range(1, X):
-            total = total + rc2[at_x(-k)[0]]
-        sc2[...] = total
-
-    for k in range(1, Y):
-        p, to = at_y(k)
-        ph, pw = yhl(p)
-        rsc3[k] = send(sc2.at[pw, ph], rc3.at[y], to, even)
     products(4, 8)
     valo[...] = acc[...].astype(BF16)
 

time: 67.7 us -> 64.8 us (0.957)
  Pallas kernels: 66.1 us -> 63.3 us
    pallas_call x1, Pallas kernels: 63.3 us -> 60.5 us  [shards(): pl.pallas_call(functools.partial(kernel, scale), out_shape=tuple((pltpu.V...]
where the time goes in v4:
time: 64.8 us; the launch traced here: 63.9 us
  Pallas kernels  63.3 us (98%)
    pallas_call x1, Pallas kernels, shards(): pl.pallas_call(functools.partial(kernel, scale), out_shape=tuple((pltpu.V...  60.5 us
    pallas_call x1, Pallas kernels, shards(): pl.pallas_call(write_kernel, out_shape=tuple((jax.ShapeDtypeStruct(s, d)...  2.84 us

profile of v4, /device:TPU:8, one launch (start us, length us, event | category | flops | bytes accessed | tf_op | source)
XLA Modules:
  0.0 63.9 jit_solution(5721318920670420518)
XLA Ops:
  0.6 60.5 %gather_scatter.1 = (bf16[704,512]{1,0:T(8,128)(2,1)S(1)}, bf16[704,4096]{1,0:T(8,128)(2,1)S(1)}, f32[16,512]{1,0:T(8,128)S(1)}, f32[1,512]{1,0:T(1,128)S(1)}) custom-call(bf16[704,4096]{1,0:T(8,128)(2,1)} %tok_hbm.1, bf16[16,512]{1,0:T(8,128)(2,1)} %w_hbm.1, f32[1,512]{1,0:T(1,128)} %bitcast.2, bf16[704,512]{1,0:T(8,128)(2,1)} %gv_hbm.1), custom_call_target="tpu_custom_call" | custom-call | flops 8858370048 | bytes 11534336 | tf_op jit(solution)/shard_map/gather_scatter/pallas_call | solution.py:579
  61.1 2.8 %write.1 = (bf16[704,512]{1,0:T(8,128)(2,1)}, bf16[704,4096]{1,0:T(8,128)(2,1)}, f32[16,512]{1,0:T(8,128)}, f32[1,512]{1,0:T(1,128)}) custom-call(bf16[704,512]{1,0:T(8,128)(2,1)S(1)} %get-tuple-element.12.val, bf16[704,4096]{1,0:T(8,128)(2,1)S(1)} %get-tuple-element.13.gt, f32[16,512]{1,0:T(8,128)S(1)} %get-tuple-element.14.gw, ...), custom_call_target="tpu_custom_call" | custom-call | tf_op jit(solution)/shard_map/write/pallas_call | solution.py:594

commit v5 on v4

--- a/solution.py
+++ b/solution.py
@@ -156,8 +156,8 @@
             device_id=sibling, device_id_type=MESH,
         )
 
-    def grads(h):
-        @pl.loop(0, Z)
+    def grads(h, lo, hi):
+        @pl.loop(lo, hi)
         def _(i):
             col = pl.multiple_of((half[h] * Z + reversed_bits(i)) * 256, 256)
             part = lax.dot_general(
@@ -185,7 +185,9 @@
 
     gv_in.wait()
     tok_in[0].wait()
-    grads(0)
+    grads(0, 0, Z)
+    tok_in[1].wait()
+    grads(1, 0, 4)
 
     def combine(h):
         def add(i, top):
@@ -259,42 +261,42 @@
         ref = wb.at[:, pz, c, :, x, G3]
         agc2[k] = send(ref, ref, at_x(k)[1], even)
 
-    def spread_a(m):
-        for k in range(1, X):
+    def spread_a(m, ks):
+        for k in ks:
             for q in range(2):
                 ref = a_piece(at_y(-m)[0], x, q)
                 ag3a[k, q, m] = send(ref, ref, at_x(k)[1])
 
-    def spread_b(m):
-        for k in range(1, Y):
+    def spread_b(m, ks):
+        for k in ks:
             for q in range(3):
                 ref = b_piece(y, at_x(-m)[0], q)
                 ag3b[k, q, m] = send(ref, ref, at_y(k)[1])
 
-    spread_a(0)
-    spread_b(0)
-
-    tok_in[1].wait()
-    grads(1)
+    spread_a(0, (1, 3, 2))
+    spread_b(0, (1, 3, 2))
+
+    grads(1, 4, Z)
     gvf = gv[...].astype(F32)
     bb[c] = jnp.sum(gvf.reshape(-1, 8, 512), axis=0)
     bias_core = send(bb.at[c], bb.at[c], sibling)
 
+    for k in range(1, X):
+        got(agc2[k], wb.at[:, pz, c, :, at_x(-k)[0], G3], even)
+    c_slab = lambda p: wb.at[:, reversed_bits(p), c, :, :, G3]
+    for k in range(1, Z):
+        ag3c[k] = send(c_slab(z), c_slab(z), at_z(k)[1], even)
+
     combine(1)
     scatter_first(1)
 
     for m in range(1, X):
         for q in range(2):
             got(ag2a[m, q], a_piece(at_y(-m)[0], x, q))
-        spread_a(m)
+        spread_a(m, (1, 3))
         for q in range(3):
             got(ag2b[m, q], b_piece(y, at_x(-m)[0], q))
-        spread_b(m)
-    for k in range(1, X):
-        got(agc2[k], wb.at[:, pz, c, :, at_x(-k)[0], G3], even)
-    c_slab = lambda p: wb.at[:, reversed_bits(p), c, :, :, G3]
-    for k in range(1, Z):
-        ag3c[k] = send(c_slab(z), c_slab(z), at_z(k)[1], even)
+        spread_b(m, (1, 3))
 
     got(bias_core, bb.at[1 - c])
     bx[x] = bb[0] + bb[1]
@@ -325,6 +327,9 @@
 
     second_a(0)
     second_a(1)
+    for m in range(1, X):
+        spread_a(m, (2,))
+        spread_b(m, (2,))
     top = jnp.full((8, 128), LEAST, F32)
     for k in range(1, Y):
         got(rsu["y", k], uy.at[at_y(-k)[0]])
@@ -373,7 +378,7 @@
         relay_a[0, q] = relay(a_slab(x, q, c))
     for q in range(3):
         relay_b[0, q] = relay(b_slab(y, q, c))
-    for k in range(1, X):
+    for k in (1, 3, 2):
         for q in range(2):
             for m in range(Y):
                 got(ag3a[k, q, m], a_piece(at_y(-m)[0], at_x(-k)[0], q))

time: 64.8 us -> 65.7 us (1.014)
  the two profiles are of different devices: /device:TPU:8 before, /device:TPU:1 now
where the time goes in v5:
time: 65.7 us; the launch traced here: 65.6 us
  Pallas kernels  65 us (99%)
    pallas_call x1, Pallas kernels, shards(): pl.pallas_call(functools.partial(kernel, scale), out_shape=tuple((pltpu.V...  62.2 us
    pallas_call x1, Pallas kernels, shards(): pl.pallas_call(write_kernel, out_shape=tuple((jax.ShapeDtypeStruct(s, d)...  2.84 us

profile of v5, /device:TPU:1, one launch (start us, length us, event | category | flops | bytes accessed | tf_op | source)
XLA Modules:
  0.0 65.6 jit_solution(3148824183859235364)
XLA Ops:
  0.6 62.2 %gather_scatter.1 = (bf16[704,512]{1,0:T(8,128)(2,1)S(1)}, bf16[704,4096]{1,0:T(8,128)(2,1)S(1)}, f32[16,512]{1,0:T(8,128)S(1)}, f32[1,512]{1,0:T(1,128)S(1)}) custom-call(bf16[704,4096]{1,0:T(8,128)(2,1)} %tok_hbm.1, bf16[16,512]{1,0:T(8,128)(2,1)} %w_hbm.1, f32[1,512]{1,0:T(1,128)} %bitcast.2, bf16[704,512]{1,0:T(8,128)(2,1)} %gv_hbm.1), custom_call_target="tpu_custom_call" | custom-call | flops 8858370048 | bytes 11534336 | tf_op jit(solution)/shard_map/gather_scatter/pallas_call | solution.py:584
  62.8 2.8 %write.1 = (bf16[704,512]{1,0:T(8,128)(2,1)}, bf16[704,4096]{1,0:T(8,128)(2,1)}, f32[16,512]{1,0:T(8,128)}, f32[1,512]{1,0:T(1,128)}) custom-call(bf16[704,512]{1,0:T(8,128)(2,1)S(1)} %get-tuple-element.12.val, bf16[704,4096]{1,0:T(8,128)(2,1)S(1)} %get-tuple-element.13.gt, f32[16,512]{1,0:T(8,128)S(1)} %get-tuple-element.14.gw, ...), custom_call_target="tpu_custom_call" | custom-call | tf_op jit(solution)/shard_map/write/pallas_call | solution.py:599

commit v6 on v5

--- a/solution.py
+++ b/solution.py
@@ -125,6 +125,13 @@
             device_id=sibling, device_id_type=MESH,
         )
         only(when, lambda: cp_.wait_recv())
+
+    drained = [0]
+
+    def drain(end):
+        for cp_, when in sends[drained[0]:end]:
+            only(when, lambda: cp_.wait_send())
+        drained[0] = end
 
     half = (1 - yl, yl)
     tok_in = []
@@ -225,12 +232,12 @@
                     code.at[half[h], zs, yhl(p)[0], :, gs], ry1.at[y, zs, :, ls], to
                 )
             rsu["y", k] = send(u.at[h], uy.at[y], to)
-        for k in range(1, Z):
+        for k in range(1, Z) if h == 1 else ():
             p, to = at_z(k)
-            rsz[k, h] = send(
-                code.at[half[h], reversed_bits(p), :, :, G3], rz1.at[z, half[h]], to, away(k)[0]
+            rsz[k] = send(
+                code.at[:, reversed_bits(p), :, :, G3], rz1.at[z], to, away(k)[0]
             )
-            rsu["z", k, h] = send(u.at[h], uz.at[z, half[h]], to, away(k)[0])
+            rsu["z", k] = send(u, uz.at[z], to, away(k)[0])
 
     combine(0)
     scatter_first(0)
@@ -247,11 +254,11 @@
     ]
     ag2a, ag2b, agc2, ag3a, ag3b, ag3c = {}, {}, {}, {}, {}, {}
     for k in range(1, Y):
-        for q in range(2):
+        for q in range(len(A_PARTS)):
             ref = a_piece(y, x, q)
             ag2a[k, q] = send(ref, ref, at_y(k)[1])
     for k in range(1, X):
-        for q in range(3):
+        for q in range(len(B_PARTS)):
             ref = b_piece(y, x, q)
             ag2b[k, q] = send(ref, ref, at_x(k)[1])
     for k in range(1, Y):
@@ -261,46 +268,35 @@
         ref = wb.at[:, pz, c, :, x, G3]
         agc2[k] = send(ref, ref, at_x(k)[1], even)
 
-    def spread_a(m, ks):
-        for k in ks:
-            for q in range(2):
-                ref = a_piece(at_y(-m)[0], x, q)
-                ag3a[k, q, m] = send(ref, ref, at_x(k)[1])
-
-    def spread_b(m, ks):
-        for k in ks:
-            for q in range(3):
-                ref = b_piece(y, at_x(-m)[0], q)
-                ag3b[k, q, m] = send(ref, ref, at_y(k)[1])
-
-    spread_a(0, (1, 3, 2))
-    spread_b(0, (1, 3, 2))
+    a_slab = lambda p, q, cc: wb.at[:, A_PARTS[q][0], cc, :, p, A_PARTS[q][1]]
+    b_slab = lambda p, q, cc: wb.at[yhl(p)[1], B_PARTS[q][0], cc, yhl(p)[0], :, B_PARTS[q][1]]
+    early = len(sends)
 
     grads(1, 4, Z)
-    gvf = gv[...].astype(F32)
-    bb[c] = jnp.sum(gvf.reshape(-1, 8, 512), axis=0)
-    bias_core = send(bb.at[c], bb.at[c], sibling)
+
+    combine(1)
+    scatter_first(1)
 
     for k in range(1, X):
         got(agc2[k], wb.at[:, pz, c, :, at_x(-k)[0], G3], even)
     c_slab = lambda p: wb.at[:, reversed_bits(p), c, :, :, G3]
     for k in range(1, Z):
         ag3c[k] = send(c_slab(z), c_slab(z), at_z(k)[1], even)
-
-    combine(1)
-    scatter_first(1)
-
+    for m in range(1, Y):
+        for q in range(len(A_PARTS)):
+            got(ag2a[m, q], a_piece(at_y(-m)[0], x, q))
+    for k in range(1, X):
+        for q in range(len(A_PARTS)):
+            ag3a[k, q] = send(a_slab(x, q, c), a_slab(x, q, c), at_x(k)[1])
     for m in range(1, X):
-        for q in range(2):
-            got(ag2a[m, q], a_piece(at_y(-m)[0], x, q))
-        spread_a(m, (1, 3))
-        for q in range(3):
+        for q in range(len(B_PARTS)):
             got(ag2b[m, q], b_piece(y, at_x(-m)[0], q))
-        spread_b(m, (1, 3))
-
-    got(bias_core, bb.at[1 - c])
-    bx[x] = bb[0] + bb[1]
-    bias_x = [send(bx.at[x], bx.at[x], at_x(k)[1]) for k in range(1, X)]
+    for k in range(1, Y):
+        for q in range(len(B_PARTS)):
+            ag3b[k, q] = send(b_slab(y, q, c), b_slab(y, q, c), at_y(k)[1])
+
+    bb[c] = jnp.dot(jnp.ones((8, gv.shape[0]), BF16), gv[...], preferred_element_type=F32)
+    bias_core = send(bb.at[c], bb.at[c], sibling)
 
     rs2a, rs2b, rsc2 = {}, {}, {}
 
@@ -326,10 +322,8 @@
             rsu["y2", k] = send(u2.at[h], u2y.at[y], to)
 
     second_a(0)
+    drain(early)
     second_a(1)
-    for m in range(1, X):
-        spread_a(m, (2,))
-        spread_b(m, (2,))
     top = jnp.full((8, 128), LEAST, F32)
     for k in range(1, Y):
         got(rsu["y", k], uy.at[at_y(-k)[0]])
@@ -350,42 +344,43 @@
             rs2b[k, q] = send(eb.at[zs, p, ls], rx2.at[x, zs, ls], to)
         rsu["x2", k] = send(u2.at[2], u2x.at[x], to)
     for k in range(1, Z):
-        for h in range(2):
-            got(rsz[k, h], rz1.at[at_z(-k)[0], half[h]], even)
-            got(rsu["z", k, h], uz.at[at_z(-k)[0], half[h]], even)
+        got(rsz[k], rz1.at[at_z(-k)[0]], even)
+        got(rsu["z", k], uz.at[at_z(-k)[0]], even)
 
     @pl.when(even)
     def _():
-        for w in range(2):
-            total = gall[c, w, pz, :, :, G3]
+        for h in range(2):
+            total = gall[c, half[h], pz, :, :, G3]
             for k in range(1, Z):
                 src = at_z(-k)[0]
-                total = total + decode(rz1[src, w], uz[src, w])
-            sc[w] = total
+                total = total + decode(rz1[src, half[h]], uz[src, h])
+            sc[half[h]] = total
 
     for k in range(1, X):
         p, to = at_x(k)
         rsc2[k] = send(sc.at[:, :, p], rc2.at[x], to, even)
 
-    a_slab = lambda p, q, cc: wb.at[:, A_PARTS[q][0], cc, :, p, A_PARTS[q][1]]
-    b_slab = lambda p, q, cc: wb.at[yhl(p)[1], B_PARTS[q][0], cc, yhl(p)[0], :, B_PARTS[q][1]]
+    got(bias_core, bb.at[1 - c])
+    bx[x] = bb[0] + bb[1]
+    bias_x = [send(bx.at[x], bx.at[x], at_x(k)[1]) for k in range(1, X)]
+
+    early = len(sends)
+
     relay_a, relay_b = {}, {}
 
     def relay(ref):
         return send(ref, ref, sibling)
 
-    for q in range(2):
+    for q in range(len(A_PARTS)):
         relay_a[0, q] = relay(a_slab(x, q, c))
-    for q in range(3):
+    for q in range(len(B_PARTS)):
         relay_b[0, q] = relay(b_slab(y, q, c))
     for k in (1, 3, 2):
-        for q in range(2):
-            for m in range(Y):
-                got(ag3a[k, q, m], a_piece(at_y(-m)[0], at_x(-k)[0], q))
+        for q in range(len(A_PARTS)):
+            got(ag3a[k, q], a_slab(at_x(-k)[0], q, c))
             relay_a[k, q] = relay(a_slab(at_x(-k)[0], q, c))
-        for q in range(3):
-            for m in range(X):
-                got(ag3b[k, q, m], b_piece(at_y(-k)[0], at_x(-m)[0], q))
+        for q in range(len(B_PARTS)):
+            got(ag3b[k, q], b_slab(at_y(-k)[0], q, c))
             relay_b[k, q] = relay(b_slab(at_y(-k)[0], q, c))
     for k in range(1, Z):
         got(ag3c[k], c_slab(at_z(-k)[0]), away(k)[0])
@@ -396,6 +391,15 @@
         got(bias_x[k - 1], bx.at[at_x(-k)[0]])
     by[y] = (bx[0] + bx[1]) + (bx[2] + bx[3])
     bias_y = [send(by.at[y], by.at[y], at_y(k)[1]) for k in range(1, Y)]
+
+    drain(early)
+
+    @pl.loop(0, 2 * Z)
+    def _(i):
+        pltpu.make_async_remote_copy(
+            src_ref=gr.at[0, 0], dst_ref=gr.at[0, 0], send_sem=dsem.at[i], recv_sem=drsem.at[i],
+            device_id=sibling, device_id_type=MESH,
+        ).wait_send()
 
     for k in range(1, Y):
         got(rsu["y2", k], u2y.at[at_y(-k)[0]])
@@ -437,9 +441,9 @@
         ph, pw = yhl(p)
         rsc3[k] = send(sc2.at[pw, ph], rc3.at[y], to, even)
     for k in range(X):
-        for q in range(2):
+        for q in range(len(A_PARTS)):
             got(relay_a[k, q], a_slab(at_x(-k)[0], q, 1 - c))
-        for q in range(3):
+        for q in range(len(B_PARTS)):
             got(relay_b[k, q], b_slab(at_y(-k)[0], q, 1 - c))
     got(relay_c, c_all(1 - c))
     acc[...] = jnp.broadcast_to(bias_ref[...], acc.shape)
@@ -478,7 +482,7 @@
     total = bz[0]
     for k in range(1, Z):
         total = total + bz[k]
-    gb_ref[...] = jnp.sum(total, axis=0, keepdims=True) * scale
+    gb_ref[...] = total[0:1] * scale
     for k in range(1, Y):
         got(rsc3[k], rc3.at[at_y(-k)[0]], even)
 
@@ -505,15 +509,7 @@
             total = total + rz3[at_z(-k)[0], 3]
         gw_ref[:, pl.ds(384, 128)] = total
 
-    for cp_, when in sends:
-        only(when, lambda: cp_.wait_send())
-
-    @pl.loop(0, 2 * Z)
-    def _(i):
-        pltpu.make_async_remote_copy(
-            src_ref=gr.at[0, 0], dst_ref=gr.at[0, 0], send_sem=dsem.at[i], recv_sem=drsem.at[i],
-            device_id=sibling, device_id_type=MESH,
-        ).wait_send()
+    drain(len(sends))
     assert count[0] <= N_SEM, count[0]
 
 

time: 65.7 us -> 64.4 us (0.980)
  the two profiles are of different devices: /device:TPU:1 before, /device:TPU:8 now
where the time goes in v6:
time: 64.4 us; the launch traced here: 64.3 us
  Pallas kernels  63.6 us (99%)
    pallas_call x1, Pallas kernels, shards(): pl.pallas_call(functools.partial(kernel, scale), out_shape=tuple((pltpu.V...  60.8 us
    pallas_call x1, Pallas kernels, shards(): pl.pallas_call(write_kernel, out_shape=tuple((jax.ShapeDtypeStruct(s, d)...  2.84 us

profile of v6, /device:TPU:8, one launch (start us, length us, event | category | flops | bytes accessed | tf_op | source)
XLA Modules:
  0.0 64.3 jit_solution(13571497445864625641)
XLA Ops:
  0.6 60.8 %gather_scatter.1 = (bf16[704,512]{1,0:T(8,128)(2,1)S(1)}, bf16[704,4096]{1,0:T(8,128)(2,1)S(1)}, f32[16,512]{1,0:T(8,128)S(1)}, f32[1,512]{1,0:T(1,128)S(1)}) custom-call(bf16[704,4096]{1,0:T(8,128)(2,1)} %tok_hbm.1, bf16[16,512]{1,0:T(8,128)(2,1)} %w_hbm.1, f32[1,512]{1,0:T(1,128)} %bitcast.2, bf16[704,512]{1,0:T(8,128)(2,1)} %gv_hbm.1), custom_call_target="tpu_custom_call" | custom-call | flops 8858370048 | bytes 11534336 | tf_op jit(solution)/shard_map/gather_scatter/pallas_call | solution.py:580
  61.4 2.8 %write.1 = (bf16[704,512]{1,0:T(8,128)(2,1)}, bf16[704,4096]{1,0:T(8,128)(2,1)}, f32[16,512]{1,0:T(8,128)}, f32[1,512]{1,0:T(1,128)}) custom-call(bf16[704,512]{1,0:T(8,128)(2,1)S(1)} %get-tuple-element.12.val, bf16[704,4096]{1,0:T(8,128)(2,1)S(1)} %get-tuple-element.13.gt, f32[16,512]{1,0:T(8,128)S(1)} %get-tuple-element.14.gw, ...), custom_call_target="tpu_custom_call" | custom-call | tf_op jit(solution)/shard_map/write/pallas_call | solution.py:595

commit v7 on v6

--- a/solution.py
+++ b/solution.py
@@ -343,23 +343,6 @@
         for q, (zs, gs, ls) in enumerate(B_PARTS):
             rs2b[k, q] = send(eb.at[zs, p, ls], rx2.at[x, zs, ls], to)
         rsu["x2", k] = send(u2.at[2], u2x.at[x], to)
-    for k in range(1, Z):
-        got(rsz[k], rz1.at[at_z(-k)[0]], even)
-        got(rsu["z", k], uz.at[at_z(-k)[0]], even)
-
-    @pl.when(even)
-    def _():
-        for h in range(2):
-            total = gall[c, half[h], pz, :, :, G3]
-            for k in range(1, Z):
-                src = at_z(-k)[0]
-                total = total + decode(rz1[src, half[h]], uz[src, h])
-            sc[half[h]] = total
-
-    for k in range(1, X):
-        p, to = at_x(k)
-        rsc2[k] = send(sc.at[:, :, p], rc2.at[x], to, even)
-
     got(bias_core, bb.at[1 - c])
     bx[x] = bb[0] + bb[1]
     bias_x = [send(bx.at[x], bx.at[x], at_x(k)[1]) for k in range(1, X)]
@@ -391,6 +374,23 @@
         got(bias_x[k - 1], bx.at[at_x(-k)[0]])
     by[y] = (bx[0] + bx[1]) + (bx[2] + bx[3])
     bias_y = [send(by.at[y], by.at[y], at_y(k)[1]) for k in range(1, Y)]
+
+    for k in range(1, Z):
+        got(rsz[k], rz1.at[at_z(-k)[0]], even)
+        got(rsu["z", k], uz.at[at_z(-k)[0]], even)
+
+    @pl.when(even)
+    def _():
+        for h in range(2):
+            total = gall[c, half[h], pz, :, :, G3]
+            for k in range(1, Z):
+                src = at_z(-k)[0]
+                total = total + decode(rz1[src, half[h]], uz[src, h])
+            sc[half[h]] = total
+
+    for k in range(1, X):
+        p, to = at_x(k)
+        rsc2[k] = send(sc.at[:, :, p], rc2.at[x], to, even)
 
     drain(early)
 

time: 64.4 us -> 65.6 us (1.019)
  Pallas kernels: 63.6 us -> 64.8 us
    pallas_call x1, Pallas kernels: 60.8 us -> 62 us  [shards(): pl.pallas_call(functools.partial(kernel, scale), out_shape=tuple((pltpu.V...]
where the time goes in v7:
time: 65.6 us; the launch traced here: 65.4 us
  Pallas kernels  64.8 us (99%)
    pallas_call x1, Pallas kernels, shards(): pl.pallas_call(functools.partial(kernel, scale), out_shape=tuple((pltpu.V...  62 us
    pallas_call x1, Pallas kernels, shards(): pl.pallas_call(write_kernel, out_shape=tuple((jax.ShapeDtypeStruct(s, d)...  2.84 us

profile of v7, /device:TPU:8, one launch (start us, length us, event | category | flops | bytes accessed | tf_op | source)
XLA Modules:
  0.0 65.4 jit_solution(8704527113525428789)
XLA Ops:
  0.6 62.0 %gather_scatter.1 = (bf16[704,512]{1,0:T(8,128)(2,1)S(1)}, bf16[704,4096]{1,0:T(8,128)(2,1)S(1)}, f32[16,512]{1,0:T(8,128)S(1)}, f32[1,512]{1,0:T(1,128)S(1)}) custom-call(bf16[704,4096]{1,0:T(8,128)(2,1)} %tok_hbm.1, bf16[16,512]{1,0:T(8,128)(2,1)} %w_hbm.1, f32[1,512]{1,0:T(1,128)} %bitcast.2, bf16[704,512]{1,0:T(8,128)(2,1)} %gv_hbm.1), custom_call_target="tpu_custom_call" | custom-call | flops 8858370048 | bytes 11534336 | tf_op jit(solution)/shard_map/gather_scatter/pallas_call | solution.py:580
  62.6 2.8 %write.1 = (bf16[704,512]{1,0:T(8,128)(2,1)}, bf16[704,4096]{1,0:T(8,128)(2,1)}, f32[16,512]{1,0:T(8,128)}, f32[1,512]{1,0:T(1,128)}) custom-call(bf16[704,512]{1,0:T(8,128)(2,1)S(1)} %get-tuple-element.12.val, bf16[704,4096]{1,0:T(8,128)(2,1)S(1)} %get-tuple-element.13.gt, f32[16,512]{1,0:T(8,128)S(1)} %get-tuple-element.14.gw, ...), custom_call_target="tpu_custom_call" | custom-call | tf_op jit(solution)/shard_map/write/pallas_call | solution.py:595
